TPU v7x, 256 devices: a whole 4x4x8 slice. The times are simulated.
256 devices in a mesh: seq: 16 (over y, x), head: 16 (over z, core).
Axes of the slice: x: 4, y: 4, z: 8, core: 2. Of those that a mesh axis runs over, the one named last changes fastest.
Arguments:
- queries: bfloat16 [16384, 4096], P('seq', 'head'), may hold values from -6 to 6
- key_states: bfloat16 [16384, 4096], P('seq', 'head'), may hold values from -6 to 6
- values: bfloat16 [16384, 4096], P('seq', 'head'), may hold values from -6 to 6
- selection: int32 [32, 32, 4], P('head', 'seq'), may hold values from 0 to 31, as said below
- out_weight: bfloat16 [4096, 2048], P('head'), may hold values from -0.09375 to 0.09375
- cotangent: bfloat16 [16384, 2048], P('seq'), may hold values from -6 to 6
Outputs:
- projected: bfloat16 [16384, 2048], P(('seq', 'head'))
- query_grad: bfloat16 [16384, 4096], P('seq', 'head')
- key_grad: bfloat16 [16384, 4096], P('seq', 'head')
- value_grad: bfloat16 [16384, 4096], P('seq', 'head')
- weight_grad: float32 [4096, 2048], P('head', 'seq')
Inputs may be any that keep to these rules, and one draw needn't show every extreme that they name: Entry selection[h, b, t] is either a block below b, the entries of one row distinct, or b itself, which chooses nothing; a row holds b only where fewer than 4 blocks are chosen. For each head, the blocks chosen by the 2 query blocks of one index of seq that lie on one other index of seq are one block at most.
All inputs are finite; a program needn't handle non-finite values.
Results may differ from a plain program's by a relative error of at most 0.022.
Values may be sent and summed in bfloat16 or wider, within the bound.
A program may use at most 192 MiB of HBM per device.

v0:
```python
import math

import jax
import jax.numpy as jnp
from jax import lax
from jax.sharding import PartitionSpec as P


def to_blocks(matrix, block_count, head_pairs):
    row_count, col_count = matrix.shape
    head_size = col_count // head_pairs
    return matrix.reshape(block_count, row_count // block_count, head_pairs, head_size).transpose(
        2, 0, 1, 3
    )


def from_blocks(blocked):
    head_pairs, block_count, block_rows, head_size = blocked.shape
    return blocked.transpose(1, 2, 0, 3).reshape(block_count * block_rows, head_pairs * head_size)


def allowed_keys(usable, block_rows, chosen_count):
    columns = (chosen_count + 1) * block_rows
    row_ids = lax.broadcasted_iota(jnp.int32, (block_rows, columns), 0)
    col_ids = lax.broadcasted_iota(jnp.int32, (block_rows, columns), 1)
    causal = (col_ids < block_rows) & (col_ids <= row_ids)
    extended = jnp.concatenate([jnp.zeros((1,), jnp.bool_), usable])
    picked = jnp.repeat(extended, block_rows)[None, :]
    return causal | picked


def softmax_weights(query_rows, key_rows, allowed, scaling):
    scores = (
        jnp.einsum("qd,kd->qk", query_rows, key_rows, preferred_element_type=jnp.float32) * scaling
    )
    scores = jnp.where(allowed, scores, -1e30)
    row_max = jnp.max(scores, axis=1, keepdims=True)
    expons = jnp.exp(scores - row_max)
    return expons / jnp.sum(expons, axis=1, keepdims=True)


def shards(queries, key_states, values, selection, out_weight, cotangent):
    seq_count = lax.axis_size("seq")
    seq_index = lax.axis_index("seq")
    head_pairs, block_count, chosen_count = selection.shape
    row_count = queries.shape[0]
    head_size = queries.shape[1] // head_pairs
    block_rows = row_count // block_count
    scaling = 1.0 / math.sqrt(head_size)
    query_blocks = to_blocks(queries, block_count, head_pairs)
    local_kv = jnp.concatenate(
        [
            to_blocks(key_states, block_count, head_pairs),
            to_blocks(values, block_count, head_pairs),
        ],
        axis=3,
    )
    block_ids = seq_index * block_count + jnp.arange(block_count, dtype=jnp.int32)
    owners = selection // block_count
    local_pos = selection % block_count
    usable = selection < block_ids[None, :, None]
    remote = usable & (owners != seq_index)
    peer_ids = jnp.arange(seq_count, dtype=jnp.int32)
    matches = remote[..., None] & (owners[..., None] == peer_ids)
    wanted = jnp.max(jnp.where(matches, local_pos[..., None], -1), axis=(1, 2))
    requested = lax.all_to_all(wanted.T, "seq", split_axis=0, concat_axis=0, tiled=True)
    head_ids = jnp.arange(head_pairs, dtype=jnp.int32)[:, None, None]
    gathered = lax.all_gather(local_kv, "seq", axis=1, tiled=True)
    chosen = gathered[head_ids, selection]
    key_sets = jnp.concatenate([local_kv[:, :, None], chosen], axis=2)
    item_count = head_pairs * block_count
    flat_sets = key_sets.reshape(item_count, chosen_count + 1, block_rows, 2 * head_size)
    flat_queries = query_blocks.reshape(item_count, block_rows, head_size)
    flat_usable = usable.reshape(item_count, chosen_count)

    def forward_item(packed):
        query_rows, key_set, usable_row = packed
        key_rows = key_set[..., :head_size].reshape(-1, head_size)
        value_rows = key_set[..., head_size:].reshape(-1, head_size)
        weights = softmax_weights(
            query_rows, key_rows, allowed_keys(usable_row, block_rows, chosen_count), scaling
        )
        weights_bf = weights.astype(jnp.bfloat16)
        return jnp.dot(weights_bf, value_rows, preferred_element_type=jnp.float32).astype(
            jnp.bfloat16
        )

    attn_flat = lax.map(forward_item, (flat_queries, flat_sets, flat_usable))
    attention = from_blocks(attn_flat.reshape(head_pairs, block_count, block_rows, head_size))
    projected = lax.psum_scatter(
        jnp.dot(attention, out_weight, preferred_element_type=jnp.float32).astype(jnp.bfloat16),
        "head",
        scatter_dimension=0,
        tiled=True,
    )
    grad_attn = jnp.einsum(
        "to,co->tc", cotangent, out_weight, preferred_element_type=jnp.float32
    ).astype(jnp.bfloat16)
    weight_part = jnp.einsum("tc,to->co", attention, cotangent, preferred_element_type=jnp.float32)
    weight_grad = lax.psum_scatter(
        weight_part.astype(jnp.bfloat16), "seq", scatter_dimension=1, tiled=True
    ).astype(jnp.float32)
    flat_grads = to_blocks(grad_attn, block_count, head_pairs).reshape(
        item_count, block_rows, head_size
    )

    def backward_item(packed):
        query_rows, key_set, usable_row, grad_rows, attn_rows = packed
        key_rows = key_set[..., :head_size].reshape(-1, head_size)
        value_rows = key_set[..., head_size:].reshape(-1, head_size)
        weights = softmax_weights(
            query_rows, key_rows, allowed_keys(usable_row, block_rows, chosen_count), scaling
        )
        weights_bf = weights.astype(jnp.bfloat16)
        grad_weights = jnp.einsum(
            "qd,kd->qk", grad_rows, value_rows, preferred_element_type=jnp.float32
        )
        row_delta = jnp.sum(
            grad_rows.astype(jnp.float32) * attn_rows.astype(jnp.float32), axis=1, keepdims=True
        )
        grad_scores = (weights * (grad_weights - row_delta)).astype(jnp.bfloat16)
        grad_query = (
            jnp.dot(grad_scores, key_rows, preferred_element_type=jnp.float32) * scaling
        ).astype(jnp.bfloat16)
        key_terms = (
            jnp.einsum("qk,qd->kd", grad_scores, query_rows, preferred_element_type=jnp.float32)
            * scaling
        )
        value_terms = jnp.einsum(
            "qk,qd->kd", weights_bf, grad_rows, preferred_element_type=jnp.float32
        )
        all_terms = jnp.concatenate([key_terms, value_terms], axis=1).reshape(
            chosen_count + 1, block_rows, 2 * head_size
        )
        return (grad_query, all_terms)

    grad_flat, term_flat = lax.map(
        backward_item, (flat_queries, flat_sets, flat_usable, flat_grads, attn_flat)
    )
    all_terms = term_flat.reshape(
        head_pairs, block_count, chosen_count + 1, block_rows, 2 * head_size
    )
    chosen_terms = all_terms[:, :, 1:].reshape(
        head_pairs, block_count * chosen_count, block_rows, 2 * head_size
    )
    near_mask = (usable & (owners == seq_index)).reshape(head_pairs, -1)
    near_pos = local_pos.reshape(head_pairs, -1)
    local_targets = jnp.arange(block_count, dtype=jnp.int32)[None, :, None]
    near_onehot = (near_mask[:, None, :] & (near_pos[:, None, :] == local_targets)).astype(
        jnp.float32
    )
    local_grads = all_terms[:, :, 0] + jnp.einsum(
        "hjc,hcxy->hjxy", near_onehot, chosen_terms, precision=lax.Precision.HIGHEST
    )
    far_onehot = (
        remote.reshape(head_pairs, -1)[..., None]
        & (owners.reshape(head_pairs, -1)[..., None] == peer_ids)
    ).astype(jnp.float32)
    outgoing_grads = jnp.einsum(
        "hco,hcxy->ohxy", far_onehot, chosen_terms, precision=lax.Precision.HIGHEST
    ).astype(jnp.bfloat16)
    returned = lax.all_to_all(outgoing_grads, "seq", split_axis=0, concat_axis=0, tiled=True)
    owner_onehot = (requested.T[:, None, :] == local_targets).astype(jnp.bfloat16)
    grad_total = local_grads + jnp.einsum(
        "hjr,rhxy->hjxy", owner_onehot, returned, preferred_element_type=jnp.float32
    )
    key_grad = from_blocks(grad_total[..., :head_size].astype(jnp.bfloat16))
    value_grad = from_blocks(grad_total[..., head_size:].astype(jnp.bfloat16))
    query_grad = from_blocks(grad_flat.reshape(head_pairs, block_count, block_rows, head_size))
    return (projected, query_grad, key_grad, value_grad, weight_grad)


def solution(mesh):
    in_specs = (
        P("seq", "head"),
        P("seq", "head"),
        P("seq", "head"),
        P("head", "seq", None),
        P("head", None),
        P("seq", None),
    )
    out_specs = (
        P(("seq", "head"), None),
        P("seq", "head"),
        P("seq", "head"),
        P("seq", "head"),
        P("head", "seq"),
    )
    return jax.shard_map(shards, mesh=mesh, in_specs=in_specs, out_specs=out_specs, check_vma=False)
```

profile of v0, /device:TPU:1, one launch (start us, length us, event | category | flops | bytes accessed | tf_op | source)
XLA Modules:
  0.0 431.5 jit_solution(153896004355387903)
XLA Ops:
  12.5 7.6 %all-to-all-start = ((s32[16,1,2]{2,1,0:T(1,128)}), s32[16,1,2]{2,1,0:T(1,128)}, u32[]{:S(2)}, u32[]{:S(2)}) async-start(s32[16,1,2]{2,1,0:T(1,128)} %copy.52), calls=%async_computation.1 | async-start | bytes 16384 | tf_op jit(solution)/shard_map/all_to_all | solution.py:66
  21.7 3.5 convolution_convert_fusion.2
  27.3 103.9 %all-gather.2.cloned.1.call-done = bf16[2,32,512,256]{3,2,1,0:T(8,128)(2,1)} async-done(((bf16[2,2,512,256]{3,2,1,0:T(8,128)(2,1)}), bf16[2,32,512,256]{3,2,1,0:T(8,128)(2,1)}) %all-gather.2.cloned.1.call-update) | async-done | bytes 16777232 | tf_op jit(solution)/shard_map/all_gather | solution.py:68
  131.2 8.6 %gather_fusion = bf16[16,512,256]{2,1,0:T(8,128)(2,1)} fusion(bf16[2,32,512,256]{3,2,1,0:T(8,128)(2,1)} %all-gather.2.cloned.1.call-done, s32[16]{0:T(128)S(1)} %reshape.117), kind=kCustom, calls=%fused_computation | custom fusion | bytes 8388736 | tf_op jit(solution)/shard_map/gather | solution.py:69
  139.9 4.9 %pad_maximum_fusion.1 = bf16[4,5,512,256]{3,2,1,0:T(8,128)(2,1)} fusion(bf16[4,4,512,256]{3,2,1,0:T(8,128)(2,1)} %bitcast.188, bf16[4,1,512,256]{3,2,1,0:T(8,128)(2,1)S(1)} %bitcast.196), kind=kLoop, calls=%fused_computation.62 | loop fusion | flops 2621440 | bytes 10485760 | tf_op jit(solution)/shard_map/concatenate | solution.py:70
  144.9 19.4 %while.22 = (s32[]{:T(128)}, bf16[4,512,128]{2,1,0:T(8,128)(2,1)S(1)}, pred[4,4]{1,0:T(4,128)(4,1)S(1)}, bf16[4,512,128]{2,1,0:T(8,128)(2,1)S(1)}, bf16[4,5,512,...) while((s32[]{:T(128)}, bf16[4,512,128]{2,1,0:T(8,128)(2,1)S(1)}, pred[4,4]{1,0:T(4,128)(4,1)S(1)}, ...), condition=%wide.region_3.4_spmd, body=%wide.region_0.3_spmd.sunk | while | flops 685573632 | bytes 22571132 | solution.py:88
  164.8 4.5 %convolution_convert_fusion.1 = bf16[256,2048]{1,0:T(8,128)(2,1)} fusion(bf16[1024,2048]{1,0:T(8,128)(2,1)} %param.15, bf16[128,8,2,128]{3,2,1,0:T(2,128)(2,1)S(1)} %bitcast.199), kind=kOutput, calls=%fused_computation.64 | convolution fusion | flops 1074266112 | bytes 5767168 | tf_op jit(solution)/shard_map/tc,to->co/dot_general | solution.py:99
  172.4 69.0 %while.23 = (s32[]{:T(128)}, bf16[4,512,128]{2,1,0:T(8,128)(2,1)}, f32[4,5,512,256]{3,2,1,0:T(8,128)}, pred[4,4]{1,0:T(4,128)(4,1)S(1)}, bf16[4,512,128]{2,1,0:T...) while((s32[]{:T(128)}, bf16[4,512,128]{2,1,0:T(8,128)(2,1)}, ...), condition=%wide.region_9.10_spmd, body=%wide.region_5.9_spmd.sunk | while | flops 1700070400 | bytes 55347368 | solution.py:137
  183.0 3.2 copy.103
  186.2 3.5 constant_dynamic-update-slice_fusion.2
  200.2 3.2 copy.103
  203.4 3.5 constant_dynamic-update-slice_fusion.2
  217.5 3.2 copy.103
  220.7 3.5 constant_dynamic-update-slice_fusion.2
  237.9 3.6 constant_dynamic-update-slice_fusion.2
  241.5 3.9 slice.37
  245.4 3.2 copy-done.1
  248.7 12.1 %convert_bitcast_fusion = bf16[16,2,512,256]{3,0,2,1:T(8,128)(2,1)} fusion(f32[2,8,512,256]{3,2,1,0:T(8,128)S(1)} %bitcast.186, s32[2,8]{1,0:T(2,128)S(1)} %copy-done.7, pred[2,8]{1,0:T(4,128)(4,1)S(1)} %copy-done.8), kind=kOutput, calls=%fused_computation.57 | convolution fusion | flops 406848000 | bytes 16777296 | tf_op jit(solution)/shard_map/hco,hcxy->ohxy/dot_general | solution.py:159
  260.8 9.6 %copy.54 = bf16[16,2,512,256]{3,2,1,0:T(8,128)(2,1)} copy(bf16[16,2,512,256]{3,0,2,1:T(8,128)(2,1)} %convert_bitcast_fusion) | data formatting | bytes 16777216 | tf_op jit(solution)/shard_map/convert_element_type | solution.py:161
  270.4 5.2 %all-to-all-start.1 = ((bf16[16,2,512,256]{3,2,1,0:T(8,128)(2,1)}), bf16[16,2,512,256]{3,2,1,0:T(8,128)(2,1)}, u32[]{:S(2)}, u32[]{:S(2)}) async-start(bf16[16,2,512,256]{3,2,1,0:T(8,128)(2,1)} %copy.54), calls=%async_computation.2 | async-start | bytes 16777216 | tf_op jit(solution)/shard_map/all_to_all | solution.py:162
  275.8 3.2 convolution_convert_fusion
  285.8 113.0 %all-to-all-done.1 = bf16[16,2,512,256]{3,2,1,0:T(8,128)(2,1)} async-done(((bf16[16,2,512,256]{3,2,1,0:T(8,128)(2,1)}), bf16[16,2,512,256]{3,2,1,0:T(8,128)(2,1)}, u32[]{:S(2)}, u32[]{:S(2)}) %all-to-all-start.1) | async-done | bytes 8388640 | tf_op jit(solution)/shard_map/all_to_all | solution.py:162
  398.8 8.4 %fusion.34 = f32[2,2,512,256]{3,1,2,0:T(2,128)S(1)} fusion(bf16[16,2,512,256]{3,2,1,0:T(8,128)(2,1)} %all-to-all-done.1, s32[2,16]{1,0:T(2,128)S(1)} %bitcast.212), kind=kOutput, calls=%fused_computation.55 | convolution fusion | flops 16777280 | bytes 10485888 | tf_op jit(solution)/shard_map/hjr,rhxy->hjxy/dot_general | solution.py:164
  407.2 13.9 %fusion.44 = bf16[2,2,512,256]{3,1,2,0:T(2,128)(2,1)S(1)} fusion(f32[2,2,512,256]{3,1,2,0:T(2,128)S(1)} %fusion.34, f32[2,2,1,512,256]{4,3,2,1,0:T(8,128)S(1)} %slice.36, f32[2,8,512,256]{3,2,1,0:T(8,128)} %bitcast.187, pred[2,8]{1,0:T(4,128)(4,1)S(1)} %and.53, s32[2,8]{1,0:T(2,128)S(1)} %eq.66), kind=kOutput, calls=%fused_computation.68 | convolution fusion | flops 51904576 | bytes 13631568 | tf_op jit(solution)/shard_map/hjc,hcxy->hjxy/dot_general | solution.py:152
  (166 shorter events, 87.2 us)
Async XLA Ops:
  7.2 14.6 %copy-start = (bf16[256,2048]{1,0:T(8,128)(2,1)S(1)}, bf16[256,2048]{1,0:T(8,128)(2,1)}, u32[]{:S(2)}) copy-start(bf16[256,2048]{1,0:T(8,128)(2,1)} %param.14) | copy-start | bytes 3145732
  7.2 3.8 copy-start.4
  7.2 14.3 %copy-start.3 = (bf16[1024,256]{1,0:T(8,128)(2,1)S(1)}, bf16[1024,256]{1,0:T(8,128)(2,1)}, u32[]{:S(2)}) copy-start(bf16[1024,256]{1,0:T(8,128)(2,1)} %param.10) | copy-start | bytes 1572868
  7.2 124.0 %all-gather.2.cloned.1.call-start = ((), (), s32[]{:S(2)}) async-start(), calls=%async_computation.4 | async-start | bytes 17825792 | tf_op jit(solution)/shard_map/all_gather | solution.py:68
  11.0 10.4 %copy-start.5 = (s32[2,2,4]{2,1,0:T(2,128)}, s32[2,2,4]{2,1,0:T(2,128)S(1)}, u32[]{:S(2)}) copy-start(s32[2,2,4]{2,1,0:T(2,128)S(1)} %and_select_fusion) | copy-start | bytes 196
  12.5 257.9 %all-to-all-start = ((s32[16,1,2]{2,1,0:T(1,128)}), s32[16,1,2]{2,1,0:T(1,128)}, u32[]{:S(2)}, u32[]{:S(2)}) async-start(s32[16,1,2]{2,1,0:T(1,128)} %copy.52), calls=%async_computation.1 | async-start | bytes 16384 | tf_op jit(solution)/shard_map/all_to_all | solution.py:66
  20.1 264.1 %reduce-scatter.7.cloned.1.call-start = ((), (), s32[]{:S(2)}) async-start(), calls=%async_computation.6 | async-start | bytes 1114112
  25.2 114.7 %copy-start.2 = (bf16[2,2,512,256]{3,2,1,0:T(8,128)(2,1)S(1)}, bf16[2,2,512,256]{3,2,1,0:T(8,128)(2,1)}, u32[]{:S(2)}) copy-start(bf16[2,2,512,256]{3,2,1,0:T(8,128)(2,1)} %pad_maximum_fusion.2) | copy-start | bytes 3145732
  241.5 7.2 %copy-start.7 = (s32[2,8]{1,0:T(2,128)S(1)}, s32[2,8]{1,0:T(2,128)}, u32[]{:S(2)}) copy-start(s32[2,8]{1,0:T(2,128)} %eq.76) | copy-start | bytes 196
  241.5 7.2 %copy-start.8 = (pred[2,8]{1,0:T(4,128)(4,1)S(1)}, pred[2,8]{1,0:T(4,128)(4,1)}, u32[]{:S(2)}) copy-start(pred[2,8]{1,0:T(4,128)(4,1)} %and.60) | copy-start | bytes 52
  245.4 3.2 copy-start.1
  270.4 128.4 %all-to-all-start.1 = ((bf16[16,2,512,256]{3,2,1,0:T(8,128)(2,1)}), bf16[16,2,512,256]{3,2,1,0:T(8,128)(2,1)}, u32[]{:S(2)}, u32[]{:S(2)}) async-start(bf16[16,2,512,256]{3,2,1,0:T(8,128)(2,1)} %copy.54), calls=%async_computation.2 | async-start | bytes 16777216 | tf_op jit(solution)/shard_map/all_to_all | solution.py:162
  275.6 3.5 copy-start.6
  275.6 3.6 copy-start.9
  275.6 149.1 %reduce-scatter.5.cloned.1.call-start = ((), (), s32[]{:S(2)}) async-start(), calls=%async_computation.5 | async-start | bytes 4456448 | tf_op jit(solution)/shard_map/reduce_scatter | solution.py:90
Sparse Core Ops, SparseCore 0:
  11.1 120.0 all-gather.1
  171.7 76.1 reduce-scatter.6
  279.7 63.5 reduce-scatter.4
where the time goes:
time: 436 us; the launch traced here: 431 us
  waiting for transfers between devices  217 us (50%)
  local copies, waits for them, and re-layouts  86.9 us (20%)
  matrix products  77.2 us (18%)
  other arithmetic  22.4 us (5%)
  between operations  14.2 us (3%)
  starting transfers between devices  13.1 us (3%)
    all_to_all x1, waiting for transfers between devices, shards(): lax.all_to_all(outgoing_grads, 'seq', split_axis=0, concat_axis=0, tiled=...  113 us
    all_gather x1, waiting for transfers between devices, shards(): gathered = lax.all_gather(local_kv, 'seq', axis=1, tiled=True)  104 us
    dynamic_update_slice x4, local copies, waits for them, and re-layouts, shards(): lax.map(backward_item, (flat_queries, flat_sets, flat_usable, flat_grads,...  14.2 us
    dot_general x1, matrix products, shards(): jnp.einsum('hjc,hcxy->hjxy', near_onehot, chosen_terms, precision=lax.Pre...  13.9 us
    concatenate x4, local copies, waits for them, and re-layouts, backward_item(): jnp.concatenate([key_terms, value_terms], axis=1)  12.8 us
    dot_general x1, matrix products, shards(): jnp.einsum('hco,hcxy->ohxy', far_onehot, chosen_terms, precision=lax.Prec...  12.1 us
    squeeze x16, local copies, waits for them, and re-layouts, shards(): attn_flat = lax.map(forward_item, (flat_queries, flat_sets, flat_usable))  11.3 us
    convert_element_type x1, local copies, waits for them, and re-layouts, shards(): outgoing_grads = jnp.einsum('hco,hcxy->ohxy', far_onehot, chosen_terms, p...  9.63 us
  transfers between devices with their start and end apart: 5, of which 2 were waited for; matrix products, arithmetic and copies ran while one was open for 42% of the time, Pallas kernels for 0%

commit v1 on v0

v1 whole, which is shorter than its diff:
```python
import functools
import math

import jax
import jax.numpy as jnp
from jax import lax
from jax.experimental import pallas as pl
from jax.experimental.pallas import tpu as pltpu
from jax.sharding import PartitionSpec as P

ROW = 4
HEAD = 128
PIECE = 1024
EIGHTH = 2048
BLOCK = 512
ITEMS = 4
SLOTS = 5
ALL_BLOCKS = 32
MESH = pl.DeviceIdType.MESH
VMEM_LIMIT = 60 * 1024 * 1024
ANY = pl.BlockSpec(memory_space=pl.ANY)


def place():
    seq = lax.axis_index("seq")
    head = lax.axis_index("head")
    return seq // ROW, seq % ROW, head // 2, head % 2


def remote(src, dst, send_sem, recv_sem, device):
    return pltpu.make_async_remote_copy(
        src_ref=src,
        dst_ref=dst,
        send_sem=send_sem,
        recv_sem=recv_sem,
        device_id=device,
        device_id_type=MESH,
    )


def row_partner(k):
    y, x, z, c = place()
    device = (y * ROW + 2 * c + k, 2 * z + x // 2)
    return device, (x // 2 == c) & (x % 2 == k)


def signal_row_partners(barrier):
    for k in range(2):
        device, own = row_partner(k)

        @pl.when(jnp.logical_not(own))
        def _(device=device):
            pl.semaphore_signal(barrier, inc=1, device_id=device, device_id_type=MESH)


def row_partner_count():
    y, x, z, c = place()
    return 2 - (x // 2 == c).astype(jnp.int32)


def row_start(src, dst, send_sem, recv_sem, k):
    device, own = row_partner(k)

    @pl.when(jnp.logical_not(own))
    def _():
        remote(src, dst, send_sem, recv_sem, device).start()

    @pl.when(own)
    def _():
        pltpu.make_async_copy(src, dst, recv_sem).start()


def row_wait_recv(dst, recv_sem):
    pltpu.make_async_copy(dst, dst, recv_sem).wait()


def row_wait_send(src, dst, send_sem, recv_sem, k):
    device, own = row_partner(k)

    @pl.when(jnp.logical_not(own))
    def _():
        remote(src, dst, send_sem, recv_sem, device).wait_send()


def neighbours():
    y, x, z, c = place()
    up = (lax.rem(y + 1, ROW) * ROW + x, 2 * z + c)
    down = (lax.rem(y + ROW - 1, ROW) * ROW + x, 2 * z + c)
    sibling = (y * ROW + x, 2 * z + 1 - c)
    return up, down, sibling


def meet(with_ring):
    barrier = pltpu.get_barrier_semaphore()
    signal_row_partners(barrier)
    count = row_partner_count()
    if with_ring:
        for device in neighbours():
            pl.semaphore_signal(barrier, inc=1, device_id=device, device_id_type=MESH)
        count = count + 3
    pl.semaphore_wait(barrier, count)


def gather_kernel(
    q, k, v, do, sel, qn, kn, vn, don, seln,
    row_send, row_recv, ring_send, ring_recv, far_send, far_recv, sib_send, sib_recv,
):
    y, x, z, c = place()
    up, down, sibling = neighbours()
    meet(True)
    odd = x % 2
    home = pl.multiple_of((2 * y + x // 2) * EIGHTH + odd * PIECE, PIECE)
    spot = pl.multiple_of(odd * PIECE, PIECE)

    def row_refs(t, h):
        cols = pl.ds(h * HEAD, HEAD)
        if t == 0:
            return k.at[:, cols], kn.at[pl.ds(home, PIECE)]
        if t == 1:
            return v.at[:, cols], vn.at[pl.ds(home, PIECE)]
        if t == 2:
            return q.at[:, cols], qn.at[pl.ds(spot, PIECE)]
        if t == 3:
            return do.at[:, cols], don.at[pl.ds(spot, PIECE)]
        return sel.at[h], seln.at[odd]

    for t in range(5):
        for h in range(2):
            src, dst = row_refs(t, h)
            row_start(src, dst, row_send.at[t, h], row_recv.at[t, odd], h)

    kv = (kn, vn)

    def piece(t, shift, core, j):
        quarter = lax.rem(y + shift + ROW, ROW)
        start = pl.multiple_of((2 * quarter + core) * EIGHTH + j * PIECE, PIECE)
        return kv[t].at[pl.ds(start, PIECE)]

    def sib_copy(t, m, shift, j):
        own = piece(t, shift, c, j)
        return remote(own, own, sib_send.at[t, m, j], sib_recv.at[t, m, j], sibling)

    def ring_copy(t, way, j):
        own = piece(t, 0, c, j)
        return remote(
            own, own, ring_send.at[t, way, j], ring_recv.at[t, way, j], (up, down)[way]
        )

    def far_copy(t, way):
        own = piece(t, (-1, 1)[way], c, way)
        return remote(own, own, far_send.at[t, way], far_recv.at[t, way], (up, down)[way])

    for t in range(2):
        for j in range(2):
            row_wait_recv(piece(t, 0, c, j), row_recv.at[t, j])
            ring_copy(t, j, j).start()
            ring_copy(t, 1 - j, j).start()
            sib_copy(t, 0, 0, j).start()
    for t in range(2):
        for way in range(2):
            ring_copy(t, way, way).wait_recv()
            far_copy(t, way).start()
            sib_copy(t, 1 + way, (-1, 1)[way], way).start()
        for way in range(2):
            ring_copy(t, way, 1 - way).wait_recv()
            sib_copy(t, 1 + way, (-1, 1)[way], 1 - way).start()
    for t in range(2):
        for way in range(2):
            far_copy(t, way).wait_recv()
            sib_copy(t, 3, 2, way).start()
    for t in range(2, 5):
        for j in range(2):
            if t == 2:
                dst = qn.at[pl.ds(j * PIECE, PIECE)]
            elif t == 3:
                dst = don.at[pl.ds(j * PIECE, PIECE)]
            else:
                dst = seln.at[j]
            row_wait_recv(dst, row_recv.at[t, j])
    for t in range(5):
        for h in range(2):
            src, dst = row_refs(t, h)
            row_wait_send(src, dst, row_send.at[t, h], row_recv.at[t, odd], h)
    for t in range(2):
        for way in range(2):
            far_copy(t, way).wait_send()
            for j in range(2):
                ring_copy(t, way, j).wait_send()
        for m, shift in enumerate((0, -1, 1, 2)):
            for j in range(2):
                copy = sib_copy(t, m, shift, j)
                copy.wait_send()
                copy.wait_recv()


def gather(q, k, v, do, sel):
    half = jax.ShapeDtypeStruct((EIGHTH, HEAD), jnp.bfloat16)
    whole = jax.ShapeDtypeStruct((ALL_BLOCKS * BLOCK, HEAD), jnp.bfloat16)
    dma = pltpu.SemaphoreType.DMA
    return pl.pallas_call(
        gather_kernel,
        name="gather",
        out_shape=(half, whole, whole, half, jax.ShapeDtypeStruct((2, 8, 128), jnp.int32)),
        in_specs=[ANY] * 5,
        out_specs=(ANY,) * 5,
        scratch_shapes=[
            dma((5, 2)), dma((5, 2)), dma((2, 2, 2)), dma((2, 2, 2)),
            dma((2, 2)), dma((2, 2)), dma((2, 4, 2)), dma((2, 4, 2)),
        ],
        compiler_params=pltpu.CompilerParams(collective_id=0, has_side_effects=True),
        cost_estimate=pl.CostEstimate(flops=0, bytes_accessed=100_000_000, transcendentals=0),
    )(q, k, v, do, sel)


def dot(a, b, contract):
    return lax.dot_general(a, b, (contract, ((), ())), preferred_element_type=jnp.float32)


def attention_kernel(
    sel, q, do, k, v, out, dq, dk, dv, dk_sum, dv_sum, scores, expons
):
    y, x, z, c = place()
    scaling = 1.0 / math.sqrt(HEAD)
    factor = scaling * math.log2(math.e)

    @pl.loop(0, ALL_BLOCKS)
    def _(block):
        dk_sum[block] = jnp.zeros((BLOCK, HEAD), jnp.float32)
        dv_sum[block] = jnp.zeros((BLOCK, HEAD), jnp.float32)

    @pl.loop(0, ITEMS)
    def _(item):
        block = 8 * y + 4 * c + item
        rows = pl.ds(pl.multiple_of(item * BLOCK, BLOCK), BLOCK)
        query = q[rows, :]
        grad = do[rows, :]
        query_t = query.T
        grad_t = grad.T.astype(jnp.float32)
        ids = [block] + [sel[item // 2, item % 2, t] for t in range(SLOTS - 1)]
        top = jnp.full((1, BLOCK), -1e30, jnp.float32)
        for t in range(SLOTS):
            s = dot(k[ids[t]], query_t, ((1,), (0,)))
            if t == 0:
                key_at = lax.broadcasted_iota(jnp.int32, (BLOCK, BLOCK), 0)
                query_at = lax.broadcasted_iota(jnp.int32, (BLOCK, BLOCK), 1)
                s = jnp.where(key_at <= query_at, s, -1e30)
            else:
                s = jnp.where(ids[t] < block, s, -1e30)
            scores[t] = s
            top = jnp.maximum(top, jnp.max(s, axis=0, keepdims=True))
        top = top * factor
        total = jnp.zeros((1, BLOCK), jnp.float32)
        out_t = jnp.zeros((HEAD, BLOCK), jnp.float32)
        for t in range(SLOTS):
            e = jnp.exp2(scores[t] * factor - top)
            total = total + jnp.sum(e, axis=0, keepdims=True)
            eb = e.astype(jnp.bfloat16)
            expons[t] = eb
            out_t = out_t + dot(v[ids[t]], eb, ((0,), (0,)))
        inverse = 1.0 / total
        out_t = (out_t * inverse).astype(jnp.bfloat16)
        out[rows, :] = out_t.T
        delta = jnp.sum(grad_t * out_t.astype(jnp.float32), axis=0, keepdims=True) * inverse
        scaled_t = (grad_t * inverse).astype(jnp.bfloat16)
        scaled = scaled_t.T
        dq_t = jnp.zeros((HEAD, BLOCK), jnp.float32)
        for t in range(SLOTS):
            eb = expons[t]
            dp = dot(v[ids[t]], scaled_t, ((1,), (0,)))
            ds = (eb.astype(jnp.float32) * (dp - delta)).astype(jnp.bfloat16)
            dq_t = dq_t + dot(k[ids[t]], ds, ((0,), (0,)))
            dk_sum[ids[t]] += dot(ds, query, ((1,), (0,)))
            dv_sum[ids[t]] += dot(eb, scaled, ((1,), (0,)))
        dq[rows, :] = (dq_t * scaling).astype(jnp.bfloat16).T

    @pl.loop(0, ALL_BLOCKS)
    def _(block):
        dk[block] = (dk_sum[block] * scaling).astype(jnp.bfloat16)
        dv[block] = dv_sum[block].astype(jnp.bfloat16)


def attention(sel, q, do, k, v):
    half = jax.ShapeDtypeStruct((EIGHTH, HEAD), jnp.bfloat16)
    blocks = jax.ShapeDtypeStruct((ALL_BLOCKS, BLOCK, HEAD), jnp.bfloat16)
    vmem = pl.BlockSpec(memory_space=pltpu.VMEM)
    return pl.pallas_call(
        attention_kernel,
        name="attention",
        out_shape=(half, half, blocks, blocks),
        in_specs=[pl.BlockSpec(memory_space=pltpu.SMEM)] + [vmem] * 4,
        out_specs=(vmem,) * 4,
        scratch_shapes=[
            pltpu.VMEM((ALL_BLOCKS, BLOCK, HEAD), jnp.float32),
            pltpu.VMEM((ALL_BLOCKS, BLOCK, HEAD), jnp.float32),
            pltpu.VMEM((SLOTS, BLOCK, BLOCK), jnp.float32),
            pltpu.VMEM((SLOTS, BLOCK, BLOCK), jnp.bfloat16),
        ],
        compiler_params=pltpu.CompilerParams(vmem_limit_bytes=VMEM_LIMIT),
        cost_estimate=pl.CostEstimate(
            flops=8_000_000_000, bytes_accessed=20_000_000, transcendentals=5_000_000
        ),
    )(sel, q, do, k.reshape(ALL_BLOCKS, BLOCK, HEAD), v.reshape(ALL_BLOCKS, BLOCK, HEAD))


def back_refs(src, dst, j):
    y, x, z, c = place()
    cols = pl.ds(pl.multiple_of((x % 2) * HEAD, HEAD), HEAD)
    return src.at[pl.ds(j * PIECE, PIECE)], dst.at[:, cols]


def return_kernel(out, attn, send, recv):
    y, x, z, c = place()
    odd = x % 2
    meet(False)
    for j in range(2):
        src, dst = back_refs(out, attn, j)
        row_start(src, dst, send.at[j], recv.at[odd], j)
    for h in range(2):
        row_wait_recv(attn.at[:, pl.ds(h * HEAD, HEAD)], recv.at[h])
    for j in range(2):
        src, dst = back_refs(out, attn, j)
        row_wait_send(src, dst, send.at[j], recv.at[odd], j)


def return_attention(out):
    return pl.pallas_call(
        return_kernel,
        name="return_attention",
        out_shape=jax.ShapeDtypeStruct((PIECE, 2 * HEAD), jnp.bfloat16),
        in_specs=[ANY],
        out_specs=ANY,
        scratch_shapes=[pltpu.SemaphoreType.DMA((2,)), pltpu.SemaphoreType.DMA((2,))],
        compiler_params=pltpu.CompilerParams(collective_id=1, has_side_effects=True),
        cost_estimate=pl.CostEstimate(flops=0, bytes_accessed=20_000_000, transcendentals=0),
    )(out)


SHIFTS = (0, -1, 1, 2)
STEP = 256


def reduce_kernel(
    dq, dk, dv, dq_home, dk_home, dv_home, mine, theirs, near, far,
    row_send, row_recv, load, sib_send, sib_recv, ring_send, ring_recv, far_send, far_recv,
):
    y, x, z, c = place()
    up, down, sibling = neighbours()
    odd = x % 2
    meet(True)
    parts = (dk, dv)
    homes = (dk_home, dv_home)

    def eighth(t, shift, core):
        quarter = lax.rem(y + shift + ROW, ROW)
        start = pl.multiple_of((2 * quarter + core) * EIGHTH, EIGHTH)
        return parts[t].at[pl.ds(start, EIGHTH)]

    def load_copy(t, m):
        return pltpu.make_async_copy(eighth(t, SHIFTS[m], c), mine.at[t, m], load.at[t, m])

    def sib_copy(t, m):
        return remote(
            eighth(t, SHIFTS[m], 1 - c), theirs.at[t, m],
            sib_send.at[t, m], sib_recv.at[t, m], sibling,
        )

    def half(ref, j):
        return ref.at[pl.ds(j * PIECE, PIECE)]

    def far_copy(t, way):
        return remote(
            half(mine.at[t, 3], way), far.at[t, way],
            far_send.at[t, way], far_recv.at[t, way], (up, down)[way],
        )

    def ring_copy(t, way, j):
        return remote(
            half(mine.at[t, 2 - way], j), near.at[t, way, j],
            ring_send.at[t, way, j], ring_recv.at[t, way, j], (up, down)[way],
        )

    def add_theirs(t, m):
        load_copy(t, m).wait()
        sib_copy(t, m).wait_recv()

        @pl.loop(0, EIGHTH // STEP)
        def _(i):
            rows = pl.ds(pl.multiple_of(i * STEP, STEP), STEP)
            total = mine[t, m, rows, :].astype(jnp.float32)
            total = total + theirs[t, m, rows, :].astype(jnp.float32)
            mine[t, m, rows, :] = total.astype(jnp.bfloat16)

    for m in (3, 1, 2, 0):
        for t in range(2):
            sib_copy(t, m).start()
            load_copy(t, m).start()
    for j in range(2):
        src, dst = back_refs(dq, dq_home, j)
        row_start(src, dst, row_send.at[2, j], row_recv.at[2, odd], j)

    for t in range(2):
        add_theirs(t, 3)
        for way in range(2):
            far_copy(t, way).start()
    for t in range(2):
        for way in range(2):
            add_theirs(t, 2 - way)
            ring_copy(t, way, 1 - way).start()
    for t in range(2):
        for way in range(2):
            far_copy(t, way).wait_recv()

            @pl.loop(0, PIECE // STEP)
            def _(i, t=t, way=way):
                there = pl.ds(pl.multiple_of(i * STEP, STEP), STEP)
                here = pl.ds(pl.multiple_of(way * PIECE + i * STEP, STEP), STEP)
                total = mine[t, 2 - way, here, :].astype(jnp.float32)
                total = total + far[t, way, there, :].astype(jnp.float32)
                mine[t, 2 - way, here, :] = total.astype(jnp.bfloat16)

            ring_copy(t, way, way).start()
    for t in range(2):
        load_copy(t, 0).wait()
        sib_copy(t, 0).wait_recv()
        for j in range(2):
            for way in range(2):
                ring_copy(t, way, j).wait_recv()

            @pl.loop(0, PIECE // STEP)
            def _(i, t=t, j=j):
                there = pl.ds(pl.multiple_of(i * STEP, STEP), STEP)
                here = pl.ds(pl.multiple_of(j * PIECE + i * STEP, STEP), STEP)
                total = mine[t, 0, here, :].astype(jnp.float32)
                total = total + theirs[t, 0, here, :].astype(jnp.float32)
                total = total + near[t, 0, j, there, :].astype(jnp.float32)
                total = total + near[t, 1, j, there, :].astype(jnp.float32)
                mine[t, 0, here, :] = total.astype(jnp.bfloat16)

            src, dst = back_refs(mine.at[t, 0], homes[t], j)
            row_start(src, dst, row_send.at[t, j], row_recv.at[t, odd], j)

    all_homes = homes + (dq_home,)
    for t in range(3):
        for h in range(2):
            row_wait_recv(all_homes[t].at[:, pl.ds(h * HEAD, HEAD)], row_recv.at[t, h])
        for j in range(2):
            src, dst = back_refs(mine.at[t, 0] if t < 2 else dq, all_homes[t], j)
            row_wait_send(src, dst, row_send.at[t, j], row_recv.at[t, odd], j)
    for t in range(2):
        for m in range(4):
            sib_copy(t, m).wait_send()
        for way in range(2):
            far_copy(t, way).wait_send()
            for j in range(2):
                ring_copy(t, way, j).wait_send()


def reduce_home(dq, dk, dv):
    home = jax.ShapeDtypeStruct((PIECE, 2 * HEAD), jnp.bfloat16)
    dma = pltpu.SemaphoreType.DMA
    return pl.pallas_call(
        reduce_kernel,
        name="reduce_home",
        out_shape=(home,) * 3,
        in_specs=[ANY] * 3,
        out_specs=(ANY,) * 3,
        scratch_shapes=[
            pltpu.VMEM((2, 4, EIGHTH, HEAD), jnp.bfloat16),
            pltpu.VMEM((2, 4, EIGHTH, HEAD), jnp.bfloat16),
            pltpu.VMEM((2, 2, 2, PIECE, HEAD), jnp.bfloat16),
            pltpu.VMEM((2, 2, PIECE, HEAD), jnp.bfloat16),
            dma((3, 2)), dma((3, 2)), dma((2, 4)), dma((2, 4)), dma((2, 4)),
            dma((2, 2, 2)), dma((2, 2, 2)), dma((2, 2)), dma((2, 2)),
        ],
        compiler_params=pltpu.CompilerParams(
            collective_id=2, has_side_effects=True, vmem_limit_bytes=VMEM_LIMIT
        ),
        cost_estimate=pl.CostEstimate(flops=0, bytes_accessed=150_000_000, transcendentals=0),
    )(dq, dk.reshape(-1, HEAD), dv.reshape(-1, HEAD))


def shards(queries, key_states, values, selection, out_weight, cotangent):
    grad_attn = dot(cotangent, out_weight, ((1,), (1,))).astype(jnp.bfloat16)
    sel = jnp.pad(selection, ((0, 0), (0, 6), (0, 124)))
    q, k, v, do, sel = gather(queries, key_states, values, grad_attn, sel)
    out, dq, dk, dv = attention(sel, q, do, k, v)
    attn = return_attention(out)
    part = dot(attn, out_weight, ((1,), (0,))).astype(jnp.bfloat16)
    weight_part = dot(attn, cotangent, ((0,), (0,))).astype(jnp.bfloat16)
    part, weight_part, dq = lax.optimization_barrier((part, weight_part, dq))
    projected = lax.psum_scatter(part, "head", scatter_dimension=0, tiled=True)
    weight_grad = lax.psum_scatter(weight_part, "seq", scatter_dimension=1, tiled=True)
    query_grad, key_grad, value_grad = reduce_home(dq, dk, dv)
    return projected, query_grad, key_grad, value_grad, weight_grad.astype(jnp.float32)


def solution(mesh):
    in_specs = (
        P("seq", "head"),
        P("seq", "head"),
        P("seq", "head"),
        P("head", "seq", None),
        P("head", None),
        P("seq", None),
    )
    out_specs = (
        P(("seq", "head"), None),
        P("seq", "head"),
        P("seq", "head"),
        P("seq", "head"),
        P("head", "seq"),
    )
    return jax.shard_map(shards, mesh=mesh, in_specs=in_specs, out_specs=out_specs, check_vma=False)
```

time: 436 us -> 270 us (0.62)
  Pallas kernels: 0 us -> 145 us
  waiting for transfers between devices: 217 us -> 87.1 us
  local copies, waits for them, and re-layouts: 86.9 us -> 9.25 us
  matrix products: 77.2 us -> 11.2 us
  other arithmetic: 22.4 us -> 0.67 us
  starting transfers between devices: 13.1 us -> 0.08 us
    pallas_call x0 -> x4, Pallas kernels: none -> 145 us  [the longest x1 52.8 us: gather(): pl.pallas_call(gather_kernel, name='gather', out_shape=(half, whole, whol...]
    all_to_all x2 -> x0, waiting for transfers between devices: 113 us -> none  [the longest x1 113 us: shards(): lax.all_to_all(outgoing_grads, 'seq', split_axis=0, concat_axis=0, tiled=...]
    all_gather x1 -> x0, waiting for transfers between devices: 104 us -> none  [shards(): gathered = lax.all_gather(local_kv, 'seq', axis=1, tiled=True)]
    dot_general x34 -> x3, matrix products: 77.2 us -> 11.2 us  [dot(): lax.dot_general(a, b, (contract, ((), ())), preferred_element_type=jnp.fl...]
    reduce_scatter x1, waiting for transfers between devices: 0.01 us -> 62.3 us  [shards(): projected = lax.psum_scatter(part, 'head', scatter_dimension=0, tiled=True)]
    unnamed x4 -> x3, waiting for transfers between devices: 0.05 us -> 24.8 us
    dynamic_update_slice x4 -> x0, local copies, waits for them, and re-layouts: 14.2 us -> none  [shards(): lax.map(backward_item, (flat_queries, flat_sets, flat_usable, flat_grads,...]
    concatenate x15 -> x0, other arithmetic: 13.6 us -> none  [the longest x4 6.95 us: backward_item(): jnp.concatenate([key_terms, value_terms], axis=1)]
  transfers between devices with their start and end apart: 5 -> 2, of which waited for: 2 -> 2; matrix products, arithmetic and copies ran while one was open for 42% -> 1% of each run, Pallas kernels for 0% -> 20%
where the time goes in v1:
time: 270 us; the launch traced here: 267 us
  Pallas kernels  145 us (54%)
  waiting for transfers between devices  87.1 us (32%)
  between operations  14.1 us (5%)
  matrix products  11.2 us (4%)
  local copies, waits for them, and re-layouts  9.25 us (3%)
    reduce_scatter x1, waiting for transfers between devices, shards(): projected = lax.psum_scatter(part, 'head', scatter_dimension=0, tiled=True)  62.3 us
    pallas_call x1, Pallas kernels, gather(): pl.pallas_call(gather_kernel, name='gather', out_shape=(half, whole, whol...  52.8 us
    pallas_call x1, Pallas kernels, reduce_home(): pl.pallas_call(reduce_kernel, name='reduce_home', out_shape=(home,) * 3,...  52.6 us
    pallas_call x1, Pallas kernels, attention(): pl.pallas_call(attention_kernel, name='attention', out_shape=(half, half,...  29.1 us
    unnamed x3, waiting for transfers between devices  24.8 us
    dot_general x3, matrix products, dot(): lax.dot_general(a, b, (contract, ((), ())), preferred_element_type=jnp.fl...  11.2 us
    pallas_call x1, Pallas kernels, return_attention(): pl.pallas_call(return_kernel, name='return_attention', out_shape=jax.Shap...  10.2 us
    unnamed x9, local copies, waits for them, and re-layouts  7.89 us
  transfers between devices with their start and end apart: 2, of which 2 were waited for; matrix products, arithmetic and copies ran while one was open for 1% of the time, Pallas kernels for 20%

profile of v1, /device:TPU:1, one launch (start us, length us, event | category | flops | bytes accessed | tf_op | source)
XLA Modules:
  0.0 267.2 jit_solution(17779817418541975725)
XLA Ops:
  7.2 0.0 copy-start
  7.2 0.0 reduce-scatter.7.cloned.1.call-start
  7.2 1.4 pad.4.sel
  8.6 0.0 copy-done
  8.6 4.3 %convolution_convert_fusion.2.do = bf16[1024,256]{1,0:T(8,128)(2,1)} fusion(bf16[1024,2048]{1,0:T(8,128)(2,1)} %param.11, bf16[256,2048]{1,0:T(8,128)(2,1)S(1)} %copy-done), kind=kOutput, calls=%fused_computation.2 | convolution fusion | flops 1074003968 | bytes 5767168 | tf_op jit(solution)/shard_map/dot_general | solution.py:216
  12.9 52.8 %gather.1 = (bf16[2048,128]{1,0:T(8,128)(2,1)}, bf16[16384,128]{1,0:T(8,128)(2,1)}, bf16[16384,128]{1,0:T(8,128)(2,1)}, bf16[2048,128]{1,0:T(8,128)(2,1)}, s32[2,8,128]{2,1,0:T(8,128)}) custom-call(bf16[1024,256]{1,0:T(8,128)(2,1)} %q.1, bf16[1024,256]{1,0:T(8,128)(2,1)} %k.1, bf16[1024,256]{1,0:T(8,128)(2,1)} %v.1, ...), custom_call_target="tpu_custom_call" | custom-call | bytes 100000000 | tf_op jit(solution)/shard_map/gather/pallas_call | solution.py:200
  65.7 29.1 %attention.1 = (bf16[2048,128]{1,0:T(8,128)(2,1)}, bf16[2048,128]{1,0:T(8,128)(2,1)}, bf16[32,512,128]{2,1,0:T(8,128)(2,1)}, bf16[32,512,128]{2,1,0:T(8,128)(2,1)}) custom-call(s32[2,8,128]{2,1,0:T(8,128)} %get-tuple-element.20.sel, bf16[2048,128]{1,0:T(8,128)(2,1)} %get-tuple-element.21.q, bf16[2048,128]{1,0:T(8,128)(2,1)} %get-tuple-element.22.do, ...), custom_call_target="tpu_custom_call" | custom-call | flops 8000000000 | bytes 20000000 | tf_op jit(solution)/shard_map/attention/pallas_call | solution.py:286
  94.8 10.2 %return_attention.1 = bf16[1024,256]{1,0:T(8,128)(2,1)} custom-call(bf16[2048,128]{1,0:T(8,128)(2,1)} %get-tuple-element.25.out), custom_call_target="tpu_custom_call" | custom-call | bytes 20000000 | tf_op jit(solution)/shard_map/return_attention/pallas_call | solution.py:326
  105.0 0.0 copy-start.1
  105.0 3.7 %convolution_convert_fusion.1 = bf16[256,2048]{1,0:T(8,128)(2,1)S(1)} fusion(bf16[1024,256]{1,0:T(8,128)(2,1)} %return_attention.1, bf16[1024,2048]{1,0:T(8,128)(2,1)} %param.11), kind=kOutput, calls=%fused_computation.1 | convolution fusion | flops 1074266112 | bytes 5767168 | tf_op jit(solution)/shard_map/dot_general | solution.py:216
  108.7 0.0 copy-done.1
  108.7 3.2 %convolution_convert_fusion = bf16[1024,2048]{1,0:T(8,128)(2,1)} fusion(bf16[1024,256]{1,0:T(8,128)(2,1)S(1)} %copy-done.1, bf16[256,2048]{1,0:T(8,128)(2,1)S(1)} %copy-done), kind=kOutput, calls=%fused_computation | convolution fusion | flops 1075838976 | bytes 5767168 | tf_op jit(solution)/shard_map/dot_general | solution.py:216
  111.9 1.3 copy.11
  113.2 0.0 reduce-scatter.7.cloned.1.call-update
  113.3 0.0 reduce-scatter.5.cloned.1.call-start
  113.3 0.7 reduce-scatter.5.cloned.1.call-update
  114.0 52.6 %reduce_home.1 = (bf16[1024,256]{1,0:T(8,128)(2,1)}, bf16[1024,256]{1,0:T(8,128)(2,1)}, bf16[1024,256]{1,0:T(8,128)(2,1)}) custom-call(bf16[2048,128]{1,0:T(8,128)(2,1)} %get-tuple-element.28.dq, bf16[16384,128]{1,0:T(8,128)(2,1)} %bitcast.12, bf16[16384,128]{1,0:T(8,128)(2,1)} %bitcast.13), custom_call_target="tpu_custom_call" | custom-call | bytes 150000000 | tf_op jit(solution)/shard_map/reduce_home/pallas_call | solution.py:461
  166.7 24.1 %reduce-scatter.7.cloned.1.call-done = bf16[128,256]{1,0:T(8,128)(2,1)} async-done(((bf16[2048,256]{1,0:T(8,128)(2,1)}), bf16[128,256]{1,0:T(8,128)(2,1)}) %reduce-scatter.7.cloned.1.call-update) | async-done | bytes 65552
  190.8 0.9 copy.12
  191.7 0.7 convert_element_type.15
  192.4 62.3 %reduce-scatter.5.cloned.1.call-done = bf16[64,2048]{1,0:T(8,128)(2,1)} async-done(((bf16[1024,2048]{1,0:T(8,128)(2,1)}), bf16[64,2048]{1,0:T(8,128)(2,1)}) %reduce-scatter.5.cloned.1.call-update) | async-done | bytes 262160 | tf_op jit(solution)/shard_map/reduce_scatter | solution.py:491
  254.7 1.9 copy.16
  256.6 1.9 copy.17
  258.5 1.9 copy.18
Async XLA Ops:
  7.2 1.4 copy-start
  7.2 183.6 %reduce-scatter.7.cloned.1.call-start = ((), (), s32[]{:S(2)}) async-start(), calls=%async_computation.3 | async-start | bytes 1114112
  105.0 3.7 %copy-start.1 = (bf16[1024,256]{1,0:T(8,128)(2,1)S(1)}, bf16[1024,256]{1,0:T(8,128)(2,1)}, u32[]{:S(2)}) copy-start(bf16[1024,256]{1,0:T(8,128)(2,1)} %return_attention.1) | copy-start | bytes 1572868
  113.3 141.5 %reduce-scatter.5.cloned.1.call-start = ((), (), s32[]{:S(2)}) async-start(), calls=%async_computation.2 | async-start | bytes 4456448 | tf_op jit(solution)/shard_map/reduce_scatter | solution.py:491
Sparse Core Ops, SparseCore 0:
  113.4 77.3 reduce-scatter.6
  194.1 60.5 reduce-scatter.4

commit v2 on v1

--- a/solution.py
+++ b/solution.py
@@ -90,15 +90,12 @@
     return up, down, sibling
 
 
-def meet(with_ring):
+def meet(others):
     barrier = pltpu.get_barrier_semaphore()
     signal_row_partners(barrier)
-    count = row_partner_count()
-    if with_ring:
-        for device in neighbours():
-            pl.semaphore_signal(barrier, inc=1, device_id=device, device_id_type=MESH)
-        count = count + 3
-    pl.semaphore_wait(barrier, count)
+    for device in others:
+        pl.semaphore_signal(barrier, inc=1, device_id=device, device_id_type=MESH)
+    pl.semaphore_wait(barrier, row_partner_count() + len(others))
 
 
 def gather_kernel(
@@ -107,7 +104,7 @@
 ):
     y, x, z, c = place()
     up, down, sibling = neighbours()
-    meet(True)
+    meet(neighbours())
     odd = x % 2
     home = pl.multiple_of((2 * y + x // 2) * EIGHTH + odd * PIECE, PIECE)
     spot = pl.multiple_of(odd * PIECE, PIECE)
@@ -308,47 +305,34 @@
     return src.at[pl.ds(j * PIECE, PIECE)], dst.at[:, cols]
 
 
-def return_kernel(out, attn, send, recv):
-    y, x, z, c = place()
-    odd = x % 2
-    meet(False)
-    for j in range(2):
-        src, dst = back_refs(out, attn, j)
-        row_start(src, dst, send.at[j], recv.at[odd], j)
-    for h in range(2):
-        row_wait_recv(attn.at[:, pl.ds(h * HEAD, HEAD)], recv.at[h])
-    for j in range(2):
-        src, dst = back_refs(out, attn, j)
-        row_wait_send(src, dst, send.at[j], recv.at[odd], j)
-
-
-def return_attention(out):
-    return pl.pallas_call(
-        return_kernel,
-        name="return_attention",
-        out_shape=jax.ShapeDtypeStruct((PIECE, 2 * HEAD), jnp.bfloat16),
-        in_specs=[ANY],
-        out_specs=ANY,
-        scratch_shapes=[pltpu.SemaphoreType.DMA((2,)), pltpu.SemaphoreType.DMA((2,))],
-        compiler_params=pltpu.CompilerParams(collective_id=1, has_side_effects=True),
-        cost_estimate=pl.CostEstimate(flops=0, bytes_accessed=20_000_000, transcendentals=0),
-    )(out)
-
-
 SHIFTS = (0, -1, 1, 2)
 STEP = 256
+DEPTH = 8
+CHUNK = 64
 
 
 def reduce_kernel(
-    dq, dk, dv, dq_home, dk_home, dv_home, mine, theirs, near, far,
+    out, dq, dk, dv, weight, cotangent,
+    projected, dq_home, dk_home, dv_home, weight_grad,
+    attn, mine, theirs, near, far, part, part_sib, part_in, chunks, chunk_sum, row_in, col_in,
     row_send, row_recv, load, sib_send, sib_recv, ring_send, ring_recv, far_send, far_recv,
+    part_send, part_recv, z_send, z_recv, wx_send, wx_recv, wy_send, wy_recv,
 ):
     y, x, z, c = place()
     up, down, sibling = neighbours()
     odd = x % 2
-    meet(True)
+    z_next = (y * ROW + x, 2 * lax.rem(z + 1, DEPTH) + c)
+    z_last = (y * ROW + x, 2 * lax.rem(z + DEPTH - 1, DEPTH) + c)
+    across = [(y * ROW + lax.rem(x + d, ROW), 2 * z + c) for d in range(1, ROW)]
+    along = [(lax.rem(y + d, ROW) * ROW + x, 2 * z + c) for d in range(1, ROW)]
+    meet([up, down, sibling, z_next, z_last, along[1]] + across)
     parts = (dk, dv)
-    homes = (dk_home, dv_home)
+    homes = (dk_home, dv_home, dq_home, attn)
+    sources = (mine.at[0, 0], mine.at[1, 0], dq, out)
+
+    def go_home(t, j):
+        src, dst = back_refs(sources[t], homes[t], j)
+        row_start(src, dst, row_send.at[t, j], row_recv.at[t, odd], j)
 
     def eighth(t, shift, core):
         quarter = lax.rem(y + shift + ROW, ROW)
@@ -390,61 +374,180 @@
             total = total + theirs[t, m, rows, :].astype(jnp.float32)
             mine[t, m, rows, :] = total.astype(jnp.bfloat16)
 
+    def add_far(t, way):
+        far_copy(t, way).wait_recv()
+
+        @pl.loop(0, PIECE // STEP)
+        def _(i):
+            there = pl.ds(pl.multiple_of(i * STEP, STEP), STEP)
+            here = pl.ds(pl.multiple_of(way * PIECE + i * STEP, STEP), STEP)
+            total = mine[t, 2 - way, here, :].astype(jnp.float32)
+            total = total + far[t, way, there, :].astype(jnp.float32)
+            mine[t, 2 - way, here, :] = total.astype(jnp.bfloat16)
+
+        ring_copy(t, way, way).start()
+
+    def finish(t, j):
+        for way in range(2):
+            ring_copy(t, way, j).wait_recv()
+
+        @pl.loop(0, PIECE // STEP)
+        def _(i):
+            there = pl.ds(pl.multiple_of(i * STEP, STEP), STEP)
+            here = pl.ds(pl.multiple_of(j * PIECE + i * STEP, STEP), STEP)
+            total = mine[t, 0, here, :].astype(jnp.float32)
+            total = total + theirs[t, 0, here, :].astype(jnp.float32)
+            total = total + near[t, 0, j, there, :].astype(jnp.float32)
+            total = total + near[t, 1, j, there, :].astype(jnp.float32)
+            mine[t, 0, here, :] = total.astype(jnp.bfloat16)
+
+        go_home(t, j)
+
+    def part_copy():
+        return remote(part.at[:, 1 - c], part_sib, part_send, part_recv, sibling)
+
+    def z_at(shift):
+        return lax.rem(z + shift + DEPTH, DEPTH)
+
+    def z_copy(way, step):
+        src = part.at[z_at(step if way == 0 else -step), c]
+        dst = part_in.at[way, step - 1]
+        if step == DEPTH // 2:
+            rows = pl.ds(way * (CHUNK // 2), CHUNK // 2)
+            src, dst = src.at[rows], dst.at[rows]
+        return remote(
+            src, dst, z_send.at[way, step - 1], z_recv.at[way, step - 1], (z_next, z_last)[way]
+        )
+
+    def z_step(step):
+        for way in range(2):
+            z_copy(way, step + 1).wait_recv()
+            mine_at = z_at(step if way == 0 else -step)
+            rows = pl.ds(0, CHUNK)
+            if step + 1 == DEPTH // 2:
+                rows = pl.ds(way * (CHUNK // 2), CHUNK // 2)
+            total = part[mine_at, c, rows, :].astype(jnp.float32)
+            total = total + part_in[way, step, rows, :].astype(jnp.float32)
+            part[mine_at, c, rows, :] = total.astype(jnp.bfloat16)
+            z_copy(way, step).start()
+
+    def project():
+        @pl.loop(0, 4)
+        def _(i):
+            rows = pl.ds(pl.multiple_of(i * 256, 256), 256)
+            for n in range(4):
+                cols = pl.ds(n * 512, 512)
+                tile = dot(attn[rows, :], weight[:, cols], ((1,), (0,))).astype(jnp.bfloat16)
+                for a in range(2):
+                    for b in range(2):
+                        at = (2 * a + b) * CHUNK
+                        part[2 * i + a, b, :, cols] = tile[at : at + CHUNK, :]
+
+        part_copy().start()
+
+    def project_sum():
+        part_copy().wait()
+
+        @pl.loop(0, DEPTH)
+        def _(i):
+            total = part[i, c].astype(jnp.float32) + part_sib[i].astype(jnp.float32)
+            part[i, c] = total.astype(jnp.bfloat16)
+
+        for way in range(2):
+            z_copy(way, DEPTH // 2).start()
+
+    def project_end():
+        total = part[z, c].astype(jnp.float32)
+        for way in range(2):
+            z_copy(way, 1).wait_recv()
+            total = total + part_in[way, 0].astype(jnp.float32)
+        projected[...] = total.astype(jnp.bfloat16)
+
+    def across_copy(d):
+        return remote(
+            chunks.at[lax.rem(x + d, ROW)], row_in.at[d - 1],
+            wx_send.at[d - 1], wx_recv.at[d - 1], across[d - 1],
+        )
+
+    def along_copy(d):
+        return remote(
+            chunk_sum.at[lax.rem(y + d, ROW)], col_in.at[d - 1],
+            wy_send.at[d - 1], wy_recv.at[d - 1], along[d - 1],
+        )
+
+    def weight_start():
+        attn_t = attn[...].T
+        for yy in range(ROW):
+            tile = dot(attn_t, cotangent[:, yy * 512 : (yy + 1) * 512], ((1,), (0,)))
+            for xx in range(ROW):
+                chunks[xx, yy] = tile[:, xx * 128 : (xx + 1) * 128].astype(jnp.bfloat16)
+        for d in range(1, ROW):
+            across_copy(d).start()
+
+    def weight_middle():
+        for d in range(1, ROW):
+            across_copy(d).wait_recv()
+        for yy in range(ROW):
+            total = chunks[x, yy].astype(jnp.float32)
+            for d in range(ROW - 1):
+                total = total + row_in[d, yy].astype(jnp.float32)
+            chunk_sum[yy] = total.astype(jnp.bfloat16)
+        for d in range(1, ROW):
+            along_copy(d).start()
+
+    def weight_end():
+        total = chunk_sum[y].astype(jnp.float32)
+        for d in range(1, ROW):
+            along_copy(d).wait_recv()
+            total = total + col_in[d - 1].astype(jnp.float32)
+        weight_grad[...] = total
+
+    for j in range(2):
+        go_home(3, j)
     for m in (3, 1, 2, 0):
         for t in range(2):
             sib_copy(t, m).start()
             load_copy(t, m).start()
     for j in range(2):
-        src, dst = back_refs(dq, dq_home, j)
-        row_start(src, dst, row_send.at[2, j], row_recv.at[2, odd], j)
+        go_home(2, j)
 
     for t in range(2):
         add_theirs(t, 3)
         for way in range(2):
             far_copy(t, way).start()
+    for h in range(2):
+        row_wait_recv(attn.at[:, pl.ds(h * HEAD, HEAD)], row_recv.at[3, h])
+    project()
     for t in range(2):
         for way in range(2):
             add_theirs(t, 2 - way)
             ring_copy(t, way, 1 - way).start()
-    for t in range(2):
-        for way in range(2):
-            far_copy(t, way).wait_recv()
-
-            @pl.loop(0, PIECE // STEP)
-            def _(i, t=t, way=way):
-                there = pl.ds(pl.multiple_of(i * STEP, STEP), STEP)
-                here = pl.ds(pl.multiple_of(way * PIECE + i * STEP, STEP), STEP)
-                total = mine[t, 2 - way, here, :].astype(jnp.float32)
-                total = total + far[t, way, there, :].astype(jnp.float32)
-                mine[t, 2 - way, here, :] = total.astype(jnp.bfloat16)
-
-            ring_copy(t, way, way).start()
+    project_sum()
+    weight_start()
+    for way in range(2):
+        add_far(0, way)
+    z_step(3)
+    for way in range(2):
+        add_far(1, way)
+    weight_middle()
+    z_step(2)
     for t in range(2):
         load_copy(t, 0).wait()
         sib_copy(t, 0).wait_recv()
+    finish(0, 0)
+    z_step(1)
+    finish(0, 1)
+    project_end()
+    weight_end()
+    finish(1, 0)
+    finish(1, 1)
+
+    for t in range(4):
+        if t < 3:
+            for h in range(2):
+                row_wait_recv(homes[t].at[:, pl.ds(h * HEAD, HEAD)], row_recv.at[t, h])
         for j in range(2):
-            for way in range(2):
-                ring_copy(t, way, j).wait_recv()
-
-            @pl.loop(0, PIECE // STEP)
-            def _(i, t=t, j=j):
-                there = pl.ds(pl.multiple_of(i * STEP, STEP), STEP)
-                here = pl.ds(pl.multiple_of(j * PIECE + i * STEP, STEP), STEP)
-                total = mine[t, 0, here, :].astype(jnp.float32)
-                total = total + theirs[t, 0, here, :].astype(jnp.float32)
-                total = total + near[t, 0, j, there, :].astype(jnp.float32)
-                total = total + near[t, 1, j, there, :].astype(jnp.float32)
-                mine[t, 0, here, :] = total.astype(jnp.bfloat16)
-
-            src, dst = back_refs(mine.at[t, 0], homes[t], j)
-            row_start(src, dst, row_send.at[t, j], row_recv.at[t, odd], j)
-
-    all_homes = homes + (dq_home,)
-    for t in range(3):
-        for h in range(2):
-            row_wait_recv(all_homes[t].at[:, pl.ds(h * HEAD, HEAD)], row_recv.at[t, h])
-        for j in range(2):
-            src, dst = back_refs(mine.at[t, 0] if t < 2 else dq, all_homes[t], j)
+            src, dst = back_refs(sources[t], homes[t], j)
             row_wait_send(src, dst, row_send.at[t, j], row_recv.at[t, odd], j)
     for t in range(2):
         for m in range(4):
@@ -453,30 +556,75 @@
             far_copy(t, way).wait_send()
             for j in range(2):
                 ring_copy(t, way, j).wait_send()
-
-
-def reduce_home(dq, dk, dv):
+    for step in range(1, DEPTH // 2 + 1):
+        for way in range(2):
+            z_copy(way, step).wait_send()
+    for d in range(1, ROW):
+        across_copy(d).wait_send()
+        along_copy(d).wait_send()
+
+
+def reduce_home(out, dq, dk, dv, weight, cotangent):
     home = jax.ShapeDtypeStruct((PIECE, 2 * HEAD), jnp.bfloat16)
     dma = pltpu.SemaphoreType.DMA
+    vmem = pl.BlockSpec(memory_space=pltpu.VMEM)
+    wide = weight.shape[1]
+    bf16 = jnp.bfloat16
     return pl.pallas_call(
         reduce_kernel,
         name="reduce_home",
-        out_shape=(home,) * 3,
-        in_specs=[ANY] * 3,
-        out_specs=(ANY,) * 3,
+        out_shape=(
+            jax.ShapeDtypeStruct((CHUNK, wide), bf16),
+            home, home, home,
+            jax.ShapeDtypeStruct((2 * HEAD, HEAD), jnp.float32),
+        ),
+        in_specs=[ANY] * 4 + [vmem] * 2,
+        out_specs=(vmem, ANY, ANY, ANY, vmem),
         scratch_shapes=[
-            pltpu.VMEM((2, 4, EIGHTH, HEAD), jnp.bfloat16),
-            pltpu.VMEM((2, 4, EIGHTH, HEAD), jnp.bfloat16),
-            pltpu.VMEM((2, 2, 2, PIECE, HEAD), jnp.bfloat16),
-            pltpu.VMEM((2, 2, PIECE, HEAD), jnp.bfloat16),
-            dma((3, 2)), dma((3, 2)), dma((2, 4)), dma((2, 4)), dma((2, 4)),
+            pltpu.VMEM((PIECE, 2 * HEAD), bf16),
+            pltpu.VMEM((2, 4, EIGHTH, HEAD), bf16),
+            pltpu.VMEM((2, 4, EIGHTH, HEAD), bf16),
+            pltpu.VMEM((2, 2, 2, PIECE, HEAD), bf16),
+            pltpu.VMEM((2, 2, PIECE, HEAD), bf16),
+            pltpu.VMEM((DEPTH, 2, CHUNK, wide), bf16),
+            pltpu.VMEM((DEPTH, CHUNK, wide), bf16),
+            pltpu.VMEM((2, DEPTH // 2, CHUNK, wide), bf16),
+            pltpu.VMEM((ROW, ROW, 2 * HEAD, HEAD), bf16),
+            pltpu.VMEM((ROW, 2 * HEAD, HEAD), bf16),
+            pltpu.VMEM((ROW - 1, ROW, 2 * HEAD, HEAD), bf16),
+            pltpu.VMEM((ROW - 1, 2 * HEAD, HEAD), bf16),
+            dma((4, 2)), dma((4, 2)), dma((2, 4)), dma((2, 4)), dma((2, 4)),
             dma((2, 2, 2)), dma((2, 2, 2)), dma((2, 2)), dma((2, 2)),
+            dma, dma, dma((2, 4)), dma((2, 4)), dma((3,)), dma((3,)), dma((3,)), dma((3,)),
         ],
         compiler_params=pltpu.CompilerParams(
             collective_id=2, has_side_effects=True, vmem_limit_bytes=VMEM_LIMIT
         ),
         cost_estimate=pl.CostEstimate(flops=0, bytes_accessed=150_000_000, transcendentals=0),
-    )(dq, dk.reshape(-1, HEAD), dv.reshape(-1, HEAD))
+    )(out, dq, dk.reshape(-1, HEAD), dv.reshape(-1, HEAD), weight, cotangent)
+
+
+def settle_kernel(*refs):
+    sems = refs[-1]
+    count = (len(refs) - 1) // 2
+    copies = [
+        pltpu.make_async_copy(refs[i], refs[count + i], sems.at[i]) for i in range(count)
+    ]
+    for copy in copies:
+        copy.start()
+    for copy in copies:
+        copy.wait()
+
+
+def settle(*arrays):
+    return pl.pallas_call(
+        settle_kernel,
+        name="settle",
+        out_shape=tuple(jax.ShapeDtypeStruct(a.shape, a.dtype) for a in arrays),
+        in_specs=[ANY] * len(arrays),
+        out_specs=(ANY,) * len(arrays),
+        scratch_shapes=[pltpu.SemaphoreType.DMA((len(arrays),))],
+    )(*arrays)
 
 
 def shards(queries, key_states, values, selection, out_weight, cotangent):
@@ -484,14 +632,7 @@
     sel = jnp.pad(selection, ((0, 0), (0, 6), (0, 124)))
     q, k, v, do, sel = gather(queries, key_states, values, grad_attn, sel)
     out, dq, dk, dv = attention(sel, q, do, k, v)
-    attn = return_attention(out)
-    part = dot(attn, out_weight, ((1,), (0,))).astype(jnp.bfloat16)
-    weight_part = dot(attn, cotangent, ((0,), (0,))).astype(jnp.bfloat16)
-    part, weight_part, dq = lax.optimization_barrier((part, weight_part, dq))
-    projected = lax.psum_scatter(part, "head", scatter_dimension=0, tiled=True)
-    weight_grad = lax.psum_scatter(weight_part, "seq", scatter_dimension=1, tiled=True)
-    query_grad, key_grad, value_grad = reduce_home(dq, dk, dv)
-    return projected, query_grad, key_grad, value_grad, weight_grad.astype(jnp.float32)
+    return settle(*reduce_home(out, dq, dk, dv, out_weight, cotangent))
 
 
 def solution(mesh):

time: 270 us -> 213 us (0.79)
  waiting for transfers between devices: 87.1 us -> 0 us
  Pallas kernels: 145 us -> 206 us
  between operations: 14.1 us -> 0.65 us
  local copies, waits for them, and re-layouts: 9.25 us -> 1.29 us
  matrix products: 11.2 us -> 4.57 us
    reduce_scatter x1 -> x0, waiting for transfers between devices: 62.3 us -> none  [shards(): projected = lax.psum_scatter(part, 'head', scatter_dimension=0, tiled=True)]
    pallas_call x2, Pallas kernels: 62.8 us -> 124 us  [the longest x1 63.6 us: reduce_home(): pl.pallas_call(reduce_kernel, name='reduce_home', out_shape=(jax.ShapeDty...]
    unnamed x3 -> x0, waiting for transfers between devices: 24.8 us -> none
    unnamed x9 -> x0, local copies, waits for them, and re-layouts: 7.89 us -> none
    dot_general x3 -> x1, matrix products: 11.2 us -> 4.57 us  [dot(): lax.dot_general(a, b, (contract, ((), ())), preferred_element_type=jnp.fl...]
  transfers between devices with their start and end apart: 2 -> 0, of which waited for: 2 -> 0; matrix products, arithmetic and copies ran while one was open for 1% -> 0% of each run, Pallas kernels for 20% -> 0%
where the time goes in v2:
time: 213 us
  Pallas kernels  206 us (97%)
  matrix products  4.57 us (2%)
    pallas_call x1, Pallas kernels, reduce_home(): pl.pallas_call(reduce_kernel, name='reduce_home', out_shape=(jax.ShapeDty...  63.6 us
    pallas_call x1, Pallas kernels, settle(): pl.pallas_call(settle_kernel, name='settle', out_shape=tuple((jax.ShapeDt...  60.7 us
    pallas_call x1, Pallas kernels, gather(): pl.pallas_call(gather_kernel, name='gather', out_shape=(half, whole, whol...  52.8 us
    pallas_call x1, Pallas kernels, attention(): pl.pallas_call(attention_kernel, name='attention', out_shape=(half, half,...  29.1 us
    dot_general x1, matrix products, dot(): lax.dot_general(a, b, (contract, ((), ())), preferred_element_type=jnp.fl...  4.57 us

profile of v2, /device:TPU:1, one launch (start us, length us, event | category | flops | bytes accessed | tf_op | source)
XLA Modules:
  0.0 212.8 jit_solution(90879325330483656)
XLA Ops:
  0.6 1.3 pad.4.sel
  1.9 4.6 %convolution_convert_fusion.do = bf16[1024,256]{1,0:T(8,128)(2,1)} fusion(bf16[1024,2048]{1,0:T(8,128)(2,1)} %cotangent.1, bf16[256,2048]{1,0:T(8,128)(2,1)} %weight.1), kind=kOutput, calls=%fused_computation | convolution fusion | flops 1074003968 | bytes 5767168 | tf_op jit(solution)/shard_map/dot_general | solution.py:213
  6.5 52.8 %gather.1 = (bf16[2048,128]{1,0:T(8,128)(2,1)}, bf16[16384,128]{1,0:T(8,128)(2,1)}, bf16[16384,128]{1,0:T(8,128)(2,1)}, bf16[2048,128]{1,0:T(8,128)(2,1)}, s32[2,8,128]{2,1,0:T(8,128)}) custom-call(bf16[1024,256]{1,0:T(8,128)(2,1)} %q.1, bf16[1024,256]{1,0:T(8,128)(2,1)} %k.1, bf16[1024,256]{1,0:T(8,128)(2,1)} %v.1, ...), custom_call_target="tpu_custom_call" | custom-call | bytes 100000000 | tf_op jit(solution)/shard_map/gather/pallas_call | solution.py:197
  59.3 29.1 %attention.1 = (bf16[2048,128]{1,0:T(8,128)(2,1)}, bf16[2048,128]{1,0:T(8,128)(2,1)}, bf16[32,512,128]{2,1,0:T(8,128)(2,1)}, bf16[32,512,128]{2,1,0:T(8,128)(2,1)}) custom-call(s32[2,8,128]{2,1,0:T(8,128)} %get-tuple-element.19.sel, bf16[2048,128]{1,0:T(8,128)(2,1)} %get-tuple-element.20.q, bf16[2048,128]{1,0:T(8,128)(2,1)} %get-tuple-element.21.do, ...), custom_call_target="tpu_custom_call" | custom-call | flops 8000000000 | bytes 20000000 | tf_op jit(solution)/shard_map/attention/pallas_call | solution.py:283
  88.5 63.6 %reduce_home.1 = (bf16[64,2048]{1,0:T(8,128)(2,1)}, bf16[1024,256]{1,0:T(8,128)(2,1)}, bf16[1024,256]{1,0:T(8,128)(2,1)}, bf16[1024,256]{1,0:T(8,128)(2,1)}, f32[256,128]{1,0:T(8,128)}) custom-call(bf16[2048,128]{1,0:T(8,128)(2,1)} %get-tuple-element.24.out, bf16[2048,128]{1,0:T(8,128)(2,1)} %get-tuple-element.25.dq, bf16[16384,128]{1,0:T(8,128)(2,1)} %bitcast.6, ...), custom_call_target="tpu_custom_call" | custom-call | bytes 150000000 | tf_op jit(solution)/shard_map/reduce_home/pallas_call | solution.py:573
  152.1 60.7 %settle.1 = (bf16[64,2048]{1,0:T(8,128)(2,1)}, bf16[1024,256]{1,0:T(8,128)(2,1)}, bf16[1024,256]{1,0:T(8,128)(2,1)}, bf16[1024,256]{1,0:T(8,128)(2,1)}, f32[256,128]{1,0:T(8,128)}) custom-call(bf16[64,2048]{1,0:T(8,128)(2,1)} %get-tuple-element.28.refs_0_, bf16[1024,256]{1,0:T(8,128)(2,1)} %get-tuple-element.29.refs_1_, ...), custom_call_target="tpu_custom_call" | custom-call | tf_op jit(solution)/shard_map/settle/pallas_call | solution.py:620

commit v3 on v2

--- a/solution.py
+++ b/solution.py
@@ -605,25 +605,20 @@
 
 
 def settle_kernel(*refs):
-    sems = refs[-1]
-    count = (len(refs) - 1) // 2
-    copies = [
-        pltpu.make_async_copy(refs[i], refs[count + i], sems.at[i]) for i in range(count)
-    ]
-    for copy in copies:
-        copy.start()
-    for copy in copies:
-        copy.wait()
+    count = len(refs) // 2
+    for i in range(count):
+        refs[count + i][...] = refs[i][...]
 
 
 def settle(*arrays):
+    vmem = pl.BlockSpec(memory_space=pltpu.VMEM)
     return pl.pallas_call(
         settle_kernel,
         name="settle",
         out_shape=tuple(jax.ShapeDtypeStruct(a.shape, a.dtype) for a in arrays),
-        in_specs=[ANY] * len(arrays),
-        out_specs=(ANY,) * len(arrays),
-        scratch_shapes=[pltpu.SemaphoreType.DMA((len(arrays),))],
+        in_specs=[vmem] * len(arrays),
+        out_specs=(vmem,) * len(arrays),
+        compiler_params=pltpu.CompilerParams(vmem_limit_bytes=VMEM_LIMIT),
     )(*arrays)
 
 

time: 213 us -> 155 us (0.73)
  Pallas kernels: 206 us -> 148 us
    pallas_call x1, Pallas kernels: 60.7 us -> 2.75 us  [settle(): pl.pallas_call(settle_kernel, name='settle', out_shape=tuple((jax.ShapeDt...]
where the time goes in v3:
time: 155 us
  Pallas kernels  148 us (95%)
  matrix products  4.57 us (3%)
    pallas_call x1, Pallas kernels, reduce_home(): pl.pallas_call(reduce_kernel, name='reduce_home', out_shape=(jax.ShapeDty...  63.6 us
    pallas_call x1, Pallas kernels, gather(): pl.pallas_call(gather_kernel, name='gather', out_shape=(half, whole, whol...  52.8 us
    pallas_call x1, Pallas kernels, attention(): pl.pallas_call(attention_kernel, name='attention', out_shape=(half, half,...  29.1 us
    dot_general x1, matrix products, dot(): lax.dot_general(a, b, (contract, ((), ())), preferred_element_type=jnp.fl...  4.57 us

profile of v3, /device:TPU:1, one launch (start us, length us, event | category | flops | bytes accessed | tf_op | source)
XLA Modules:
  0.0 154.9 jit_solution(3355455247305311313)
XLA Ops:
  0.6 1.3 pad.4.sel
  1.9 4.6 %convolution_convert_fusion.do = bf16[1024,256]{1,0:T(8,128)(2,1)} fusion(bf16[1024,2048]{1,0:T(8,128)(2,1)} %cotangent.1, bf16[256,2048]{1,0:T(8,128)(2,1)} %weight.1), kind=kOutput, calls=%fused_computation | convolution fusion | flops 1074003968 | bytes 5767168 | tf_op jit(solution)/shard_map/dot_general | solution.py:213
  6.5 52.8 %gather.1 = (bf16[2048,128]{1,0:T(8,128)(2,1)}, bf16[16384,128]{1,0:T(8,128)(2,1)}, bf16[16384,128]{1,0:T(8,128)(2,1)}, bf16[2048,128]{1,0:T(8,128)(2,1)}, s32[2,8,128]{2,1,0:T(8,128)}) custom-call(bf16[1024,256]{1,0:T(8,128)(2,1)} %q.1, bf16[1024,256]{1,0:T(8,128)(2,1)} %k.1, bf16[1024,256]{1,0:T(8,128)(2,1)} %v.1, ...), custom_call_target="tpu_custom_call" | custom-call | bytes 100000000 | tf_op jit(solution)/shard_map/gather/pallas_call | solution.py:197
  59.3 29.1 %attention.1 = (bf16[2048,128]{1,0:T(8,128)(2,1)}, bf16[2048,128]{1,0:T(8,128)(2,1)}, bf16[32,512,128]{2,1,0:T(8,128)(2,1)}, bf16[32,512,128]{2,1,0:T(8,128)(2,1)}) custom-call(s32[2,8,128]{2,1,0:T(8,128)} %get-tuple-element.19.sel, bf16[2048,128]{1,0:T(8,128)(2,1)} %get-tuple-element.20.q, bf16[2048,128]{1,0:T(8,128)(2,1)} %get-tuple-element.21.do, ...), custom_call_target="tpu_custom_call" | custom-call | flops 8000000000 | bytes 20000000 | tf_op jit(solution)/shard_map/attention/pallas_call | solution.py:283
  88.5 63.6 %reduce_home.1 = (bf16[64,2048]{1,0:T(8,128)(2,1)}, bf16[1024,256]{1,0:T(8,128)(2,1)}, bf16[1024,256]{1,0:T(8,128)(2,1)}, bf16[1024,256]{1,0:T(8,128)(2,1)}, f32[256,128]{1,0:T(8,128)}) custom-call(bf16[2048,128]{1,0:T(8,128)(2,1)} %get-tuple-element.24.out, bf16[2048,128]{1,0:T(8,128)(2,1)} %get-tuple-element.25.dq, bf16[16384,128]{1,0:T(8,128)(2,1)} %bitcast.6, ...), custom_call_target="tpu_custom_call" | custom-call | bytes 150000000 | tf_op jit(solution)/shard_map/reduce_home/pallas_call | solution.py:573
  152.1 2.8 %settle.1 = (bf16[64,2048]{1,0:T(8,128)(2,1)}, bf16[1024,256]{1,0:T(8,128)(2,1)}, bf16[1024,256]{1,0:T(8,128)(2,1)}, bf16[1024,256]{1,0:T(8,128)(2,1)}, f32[256,128]{1,0:T(8,128)}) custom-call(bf16[64,2048]{1,0:T(8,128)(2,1)} %get-tuple-element.28.refs_0_, bf16[1024,256]{1,0:T(8,128)(2,1)} %get-tuple-element.29.refs_1_, ...), custom_call_target="tpu_custom_call" | custom-call | tf_op jit(solution)/shard_map/settle/pallas_call | solution.py:615

commit v4 on v3

v4 whole, which is shorter than its diff:
```python
import math

import jax
import jax.numpy as jnp
from jax import lax
from jax.experimental import pallas as pl
from jax.experimental.pallas import tpu as pltpu
from jax.sharding import PartitionSpec as P

ROW = 4
DEPTH = 8
HEAD = 128
BLOCK = 512
ITEMS = 4
SLOTS = 5
ALL_BLOCKS = 32
CHUNK = 64
SHIFTS = (0, -1, 1, 2)
SCALING = 1.0 / math.sqrt(HEAD)
FACTOR = SCALING * math.log2(math.e)
MESH = pl.DeviceIdType.MESH
VMEM_LIMIT = 62 * 1024 * 1024
ANY = pl.BlockSpec(memory_space=pl.ANY)


def place():
    seq = lax.axis_index("seq")
    head = lax.axis_index("head")
    return seq // ROW, seq % ROW, head // 2, head % 2


def remote(src, dst, send_sem, recv_sem, device):
    return pltpu.make_async_remote_copy(
        src_ref=src,
        dst_ref=dst,
        send_sem=send_sem,
        recv_sem=recv_sem,
        device_id=device,
        device_id_type=MESH,
    )


def row_partner(k):
    y, x, z, c = place()
    device = (y * ROW + 2 * c + k, 2 * z + x // 2)
    return device, (x // 2 == c) & (x % 2 == k)


def row_start(src, dst, send_sem, recv_sem, k):
    device, own = row_partner(k)

    @pl.when(jnp.logical_not(own))
    def _():
        remote(src, dst, send_sem, recv_sem, device).start()

    @pl.when(own)
    def _():
        pltpu.make_async_copy(src, dst, recv_sem).start()


def row_wait_recv(dst, recv_sem):
    pltpu.make_async_copy(dst, dst, recv_sem).wait()


def row_wait_send(src, dst, send_sem, recv_sem, k):
    device, own = row_partner(k)

    @pl.when(jnp.logical_not(own))
    def _():
        remote(src, dst, send_sem, recv_sem, device).wait_send()


def meet(others):
    y, x, z, c = place()
    barrier = pltpu.get_barrier_semaphore()
    for k in range(2):
        device, own = row_partner(k)

        @pl.when(jnp.logical_not(own))
        def _(device=device):
            pl.semaphore_signal(barrier, inc=1, device_id=device, device_id_type=MESH)

    for device in others:
        pl.semaphore_signal(barrier, inc=1, device_id=device, device_id_type=MESH)
    pl.semaphore_wait(barrier, 2 - (x // 2 == c).astype(jnp.int32) + len(others))


def dot(a, b, contract):
    return lax.dot_general(a, b, (contract, ((), ())), preferred_element_type=jnp.float32)


def layer_kernel(
    q_in, k_in, v_in, sel_in, weight_in, cot_in,
    projected, dq_home, dk_home, dv_home, weight_grad, sel_land,
    k_own, v_own, weight, cot, sel, qn, kn, vn, don, scaled, expons, terms, stats,
    parts, theirs, near, far, attn, part, part_sib, part_in, chunks, chunk_sum, row_in, col_in,
    load, sel_sem, row_send, row_recv, kv_send, kv_recv, kv_far_send, kv_far_recv,
    kv_sib_send, kv_sib_recv, home_send, home_recv, sib_send, sib_recv,
    ring_send, ring_recv, far_send, far_recv,
    part_send, part_recv, z_send, z_recv, wx_send, wx_recv, wy_send, wy_recv,
):
    y, x, z, c = place()
    odd = x % 2
    f32, bf16 = jnp.float32, jnp.bfloat16
    up = (lax.rem(y + 1, ROW) * ROW + x, 2 * z + c)
    down = (lax.rem(y + ROW - 1, ROW) * ROW + x, 2 * z + c)
    sibling = (y * ROW + x, 2 * z + 1 - c)
    z_next = (y * ROW + x, 2 * lax.rem(z + 1, DEPTH) + c)
    z_last = (y * ROW + x, 2 * lax.rem(z + DEPTH - 1, DEPTH) + c)
    across = [(y * ROW + lax.rem(x + d, ROW), 2 * z + c) for d in range(1, ROW)]
    along = [(lax.rem(y + d, ROW) * ROW + x, 2 * z + c) for d in range(1, ROW)]

    loads = [
        pltpu.make_async_copy(src, dst, load.at[i])
        for i, (src, dst) in enumerate(
            ((k_in, k_own), (v_in, v_own), (cot_in, cot), (weight_in, weight))
        )
    ]
    for copy in loads:
        copy.start()
    meet([up, down, sibling, z_next, z_last, along[1]] + across)

    home_at = 4 * (2 * y + x // 2) + 2 * odd

    def row_refs(t, h):
        cols = pl.ds(h * HEAD, HEAD)
        if t == 0:
            return k_own.at[:, :, cols], kn.at[pl.ds(home_at, 2)]
        if t == 1:
            return q_in.at[:, :, cols], qn.at[pl.ds(2 * odd, 2)]
        if t == 2:
            return v_own.at[:, :, cols], vn.at[pl.ds(home_at, 2)]
        if t == 3:
            return k_own.at[:, :, cols], don.at[pl.ds(2 * odd, 2)]
        return sel_in.at[h], sel_land.at[odd]

    def row_go(t):
        for h in range(2):
            src, dst = row_refs(t, h)
            row_start(src, dst, row_send.at[t, h], row_recv.at[t, odd], h)

    def row_sent(t):
        for h in range(2):
            src, dst = row_refs(t, h)
            row_wait_send(src, dst, row_send.at[t, h], row_recv.at[t, odd], h)

    def row_arrive(t, j):
        if t == 1:
            dst = qn.at[pl.ds(2 * j, 2)]
        elif t == 3:
            dst = don.at[pl.ds(2 * j, 2)]
        elif t == 4:
            dst = sel_land.at[j]
        else:
            dst = piece(t // 2, 0, c, j)
        row_wait_recv(dst, row_recv.at[t, j])

    def piece(t, shift, core, j):
        quarter = lax.rem(y + shift + ROW, ROW)
        return (kn, vn)[t].at[pl.ds(4 * (2 * quarter + core) + 2 * j, 2)]

    def kv_sib(t, m, j):
        own = piece(t, SHIFTS[m], c, j)
        return remote(own, own, kv_sib_send.at[t, m, j], kv_sib_recv.at[t, m, j], sibling)

    def kv_ring(t, way, j):
        own = piece(t, 0, c, j)
        return remote(own, own, kv_send.at[t, way, j], kv_recv.at[t, way, j], (up, down)[way])

    def kv_far(t, way):
        own = piece(t, (-1, 1)[way], c, way)
        return remote(
            own, own, kv_far_send.at[t, way], kv_far_recv.at[t, way], (up, down)[way]
        )

    def kv_begin(t):
        for j in range(2):
            row_arrive(2 * t, j)
            kv_ring(t, j, j).start()
            kv_ring(t, 1 - j, j).start()
            kv_sib(t, 0, j).start()

    def kv_relay(t):
        for way in range(2):
            kv_ring(t, way, way).wait_recv()
            kv_far(t, way).start()
            kv_sib(t, 1 + way, way).start()

    def kv_rest(t):
        for way in range(2):
            kv_ring(t, way, 1 - way).wait_recv()
            kv_sib(t, 1 + way, 1 - way).start()

    def kv_last(t):
        for way in range(2):
            kv_far(t, way).wait_recv()
            kv_sib(t, 3, way).start()

    def kv_end(t):
        for m in range(4):
            for j in range(2):
                kv_sib(t, m, j).wait_recv()

    def gradient_rows(lo, hi):
        @pl.loop(lo, hi)
        def _(i):
            rows = pl.ds(pl.multiple_of((i % 2) * 256, 256), 256)
            tile = dot(cot[i // 2, rows, :], weight[...], ((1,), (1,)))
            k_own[i // 2, rows, :] = tile.astype(bf16)

    out, dq = don, scaled

    def item_ids(item):
        block = 8 * y + 4 * c + item
        return block, [sel[item // 2, item % 2, t] for t in range(SLOTS - 1)]

    def weigh(lo, hi):
        @pl.loop(lo, hi)
        def _(item):
            block, ids = item_ids(item)
            query_t = qn[item].T
            top = jnp.full((1, BLOCK), -1e30, f32)
            for t in range(SLOTS):
                if t == 0:
                    s = dot(kn[block], query_t, ((1,), (0,)))
                    key_at = lax.broadcasted_iota(jnp.int32, (BLOCK, BLOCK), 0)
                    query_at = lax.broadcasted_iota(jnp.int32, (BLOCK, BLOCK), 1)
                    s = jnp.where(key_at <= query_at, s, -1e30)
                else:
                    s = dot(kn[ids[t - 1]], query_t, ((1,), (0,)))
                    s = jnp.where(ids[t - 1] < block, s, -1e30)
                for n in range(ITEMS):
                    terms[n, t] = s[:, n * HEAD : (n + 1) * HEAD]
                top = jnp.maximum(top, jnp.max(s, axis=0, keepdims=True))
            top = top * FACTOR
            total = jnp.zeros((1, BLOCK), f32)
            for t in range(SLOTS):
                s = jnp.concatenate([terms[n, t] for n in range(ITEMS)], axis=1)
                e = jnp.exp2(s * FACTOR - top)
                total = total + jnp.sum(e, axis=0, keepdims=True)
                expons[item, t] = e.astype(bf16)
            stats[item] = 1.0 / total

    def value_terms():
        @pl.loop(0, ITEMS)
        def _(item):
            scaled_t = (don[item].T.astype(f32) * stats[item]).astype(bf16)
            scaled[item] = scaled_t.T
            rows = scaled[item]
            for t in range(SLOTS):
                terms[item, t] = dot(expons[item, t], rows, ((1,), (0,)))

    def attend():
        @pl.loop(0, ITEMS)
        def _(item):
            block, ids = item_ids(item)
            out_t = dot(vn[block], expons[item, 0], ((0,), (0,)))
            for t in range(1, SLOTS):
                out_t = out_t + dot(vn[ids[t - 1]], expons[item, t], ((0,), (0,)))
            out_t = (out_t * stats[item]).astype(bf16)
            product = don[item].T.astype(f32) * out_t.astype(f32)
            out[item] = out_t.T
            stats[item] = jnp.sum(product, axis=0, keepdims=True) * stats[item]

    def backward(lo, hi):
        @pl.loop(lo, hi)
        def _(item):
            block, ids = item_ids(item)
            query = qn[item]
            scaled_t = scaled[item].T
            delta = stats[item]
            dq_t = jnp.zeros((HEAD, BLOCK), f32)
            for t in range(SLOTS):
                at = block if t == 0 else ids[t - 1]
                dp = dot(vn[at], scaled_t, ((1,), (0,)))
                ds = (expons[item, t].astype(f32) * (dp - delta)).astype(bf16)
                dq_t = dq_t + dot(kn[at], ds, ((0,), (0,)))
                terms[item, t] = dot(ds, query, ((1,), (0,)))
            dq[item] = (dq_t * SCALING).astype(bf16).T

    def gather_terms(t, m):
        @pl.loop(0, 8)
        def _(i):
            target = 8 * lax.rem(y + SHIFTS[m] + ROW, ROW) + i
            total = jnp.zeros((BLOCK, HEAD), f32)
            for item in range(ITEMS):
                block, ids = item_ids(item)
                slot = jnp.int32(0)
                for s in range(SLOTS - 1):
                    slot = jnp.where(ids[s] == target, s + 1, slot)
                slot = jnp.where(target == block, 0, slot)
                chosen = (target == block) | (slot > 0)
                total = total + jnp.where(chosen, terms[item, slot], 0.0)
            if t == 0:
                total = total * SCALING
            parts[t, m, i // 4, i % 4] = total.astype(bf16)

    homes = (dk_home, dv_home, dq_home, attn)
    sources = (parts.at[0, 0, c], parts.at[1, 0, c], dq, out)

    def home_refs(t, j):
        cols = pl.ds(pl.multiple_of(odd * HEAD, HEAD), HEAD)
        return sources[t].at[pl.ds(2 * j, 2)], homes[t].at[:, :, cols]

    def go_home(t, j):
        src, dst = home_refs(t, j)
        row_start(src, dst, home_send.at[t, j], home_recv.at[t, odd], j)

    def come_home(t):
        for h in range(2):
            row_wait_recv(homes[t].at[:, :, pl.ds(h * HEAD, HEAD)], home_recv.at[t, h])

    def sib_copy(t, m):
        return remote(
            parts.at[t, m, 1 - c], theirs.at[t, m],
            sib_send.at[t, m], sib_recv.at[t, m], sibling,
        )

    def far_copy(t, way):
        return remote(
            parts.at[t, 3, c, pl.ds(2 * way, 2)], far.at[t, way],
            far_send.at[t, way], far_recv.at[t, way], (up, down)[way],
        )

    def ring_copy(t, way, j):
        return remote(
            parts.at[t, 2 - way, c, pl.ds(2 * j, 2)], near.at[t, way, j],
            ring_send.at[t, way, j], ring_recv.at[t, way, j], (up, down)[way],
        )

    def share(t):
        for m in (3, 1, 2, 0):
            gather_terms(t, m)
            sib_copy(t, m).start()

    def add_theirs(t, m):
        sib_copy(t, m).wait_recv()

        @pl.loop(0, 4)
        def _(i):
            total = parts[t, m, c, i].astype(f32) + theirs[t, m, i].astype(f32)
            parts[t, m, c, i] = total.astype(bf16)

    def back_far(t):
        add_theirs(t, 3)
        for way in range(2):
            far_copy(t, way).start()

    def back_near(t):
        for way in range(2):
            add_theirs(t, 2 - way)
            ring_copy(t, way, 1 - way).start()

    def back_sum(t):
        for way in range(2):
            far_copy(t, way).wait_recv()

            @pl.loop(0, 2)
            def _(i, way=way):
                total = parts[t, 2 - way, c, 2 * way + i].astype(f32)
                total = total + far[t, way, i].astype(f32)
                parts[t, 2 - way, c, 2 * way + i] = total.astype(bf16)

            ring_copy(t, way, way).start()

    def back_end(t):
        sib_copy(t, 0).wait_recv()
        for j in range(2):
            for way in range(2):
                ring_copy(t, way, j).wait_recv()

            @pl.loop(0, 2)
            def _(i, j=j):
                total = parts[t, 0, c, 2 * j + i].astype(f32)
                total = total + theirs[t, 0, 2 * j + i].astype(f32)
                total = total + near[t, 0, j, i].astype(f32)
                total = total + near[t, 1, j, i].astype(f32)
                parts[t, 0, c, 2 * j + i] = total.astype(bf16)

            go_home(t, j)

    def part_copy():
        return remote(part.at[:, 1 - c], part_sib, part_send, part_recv, sibling)

    def z_at(shift):
        return lax.rem(z + shift + DEPTH, DEPTH)

    def z_copy(way, step):
        src = part.at[z_at(step if way == 0 else -step), c]
        dst = part_in.at[way, step - 1]
        if step == DEPTH // 2:
            rows = pl.ds(way * (CHUNK // 2), CHUNK // 2)
            src, dst = src.at[rows], dst.at[rows]
        return remote(
            src, dst, z_send.at[way, step - 1], z_recv.at[way, step - 1], (z_next, z_last)[way]
        )

    def z_step(step):
        for way in range(2):
            z_copy(way, step + 1).wait_recv()
            mine_at = z_at(step if way == 0 else -step)
            rows = pl.ds(0, CHUNK)
            if step + 1 == DEPTH // 2:
                rows = pl.ds(way * (CHUNK // 2), CHUNK // 2)
            total = part[mine_at, c, rows, :].astype(f32)
            total = total + part_in[way, step, rows, :].astype(f32)
            part[mine_at, c, rows, :] = total.astype(bf16)
            z_copy(way, step).start()

    def project():
        @pl.loop(0, 4)
        def _(i):
            rows = pl.ds(pl.multiple_of((i % 2) * 256, 256), 256)
            for n in range(4):
                cols = pl.ds(n * 512, 512)
                tile = dot(attn[i // 2, rows, :], weight[:, cols], ((1,), (0,))).astype(bf16)
                for a in range(2):
                    for b in range(2):
                        at = (2 * a + b) * CHUNK
                        part[2 * i + a, b, :, cols] = tile[at : at + CHUNK, :]

        part_copy().start()

    def project_sum():
        part_copy().wait()

        @pl.loop(0, DEPTH)
        def _(i):
            total = part[i, c].astype(f32) + part_sib[i].astype(f32)
            part[i, c] = total.astype(bf16)

        for way in range(2):
            z_copy(way, DEPTH // 2).start()

    def project_end():
        total = part[z, c].astype(f32)
        for way in range(2):
            z_copy(way, 1).wait_recv()
            total = total + part_in[way, 0].astype(f32)
        projected[...] = total.astype(bf16)

    def across_copy(d):
        return remote(
            chunks.at[lax.rem(x + d, ROW)], row_in.at[d - 1],
            wx_send.at[d - 1], wx_recv.at[d - 1], across[d - 1],
        )

    def along_copy(d):
        return remote(
            chunk_sum.at[lax.rem(y + d, ROW)], col_in.at[d - 1],
            wy_send.at[d - 1], wy_recv.at[d - 1], along[d - 1],
        )

    def weight_start():
        first_t, second_t = attn[0].T, attn[1].T
        for yy in range(ROW):
            cols = slice(yy * 512, (yy + 1) * 512)
            tile = dot(first_t, cot[0, :, cols], ((1,), (0,)))
            tile = tile + dot(second_t, cot[1, :, cols], ((1,), (0,)))
            for xx in range(ROW):
                chunks[xx, yy] = tile[:, xx * 128 : (xx + 1) * 128].astype(bf16)
        for d in range(1, ROW):
            across_copy(d).start()

    def weight_middle():
        for d in range(1, ROW):
            across_copy(d).wait_recv()
        for yy in range(ROW):
            total = chunks[x, yy].astype(f32)
            for d in range(ROW - 1):
                total = total + row_in[d, yy].astype(f32)
            chunk_sum[yy] = total.astype(bf16)
        for d in range(1, ROW):
            along_copy(d).start()

    def weight_end():
        total = chunk_sum[y].astype(f32)
        for d in range(1, ROW):
            along_copy(d).wait_recv()
            total = total + col_in[d - 1].astype(f32)
        weight_grad[...] = total

    loads[0].wait()
    row_go(0)
    loads[1].wait()
    kv_begin(0)
    row_go(2)
    row_sent(0)
    loads[2].wait()
    loads[3].wait()
    gradient_rows(0, 4)
    kv_relay(0)
    row_go(1)
    row_go(4)
    kv_rest(0)
    row_go(3)
    kv_last(0)
    kv_begin(1)
    for j in range(2):
        row_arrive(4, j)
    sel_copy = pltpu.make_async_copy(sel_land, sel, sel_sem)
    sel_copy.start()
    for j in range(2):
        row_arrive(1, j)
    kv_end(0)
    sel_copy.wait()
    weigh(0, 4)
    kv_relay(1)
    kv_rest(1)
    for j in range(2):
        row_arrive(3, j)
    value_terms()
    share(1)
    kv_last(1)
    back_far(1)
    kv_end(1)
    attend()
    for j in range(2):
        go_home(3, j)
    back_near(1)
    backward(0, 1)
    back_sum(1)
    come_home(3)
    project()
    backward(1, 2)
    project_sum()
    backward(2, 3)
    z_step(3)
    backward(3, 4)
    share(0)
    back_far(0)
    for j in range(2):
        go_home(2, j)
    z_step(2)
    back_near(0)
    weight_start()
    back_sum(0)
    z_step(1)
    weight_middle()
    back_end(1)
    project_end()
    weight_end()
    back_end(0)

    for t in range(3):
        come_home(t)
    for t in range(1, 5):
        row_sent(t)
    for t in range(4):
        for j in range(2):
            src, dst = home_refs(t, j)
            row_wait_send(src, dst, home_send.at[t, j], home_recv.at[t, odd], j)
    for t in range(2):
        for m in range(4):
            sib_copy(t, m).wait_send()
            for j in range(2):
                kv_sib(t, m, j).wait_send()
        for way in range(2):
            far_copy(t, way).wait_send()
            kv_far(t, way).wait_send()
            for j in range(2):
                ring_copy(t, way, j).wait_send()
                kv_ring(t, way, j).wait_send()
    for step in range(1, DEPTH // 2 + 1):
        for way in range(2):
            z_copy(way, step).wait_send()
    for d in range(1, ROW):
        across_copy(d).wait_send()
        along_copy(d).wait_send()


def layer(q, k, v, sel, weight, cot):
    f32, bf16 = jnp.float32, jnp.bfloat16
    home = jax.ShapeDtypeStruct((2, BLOCK, 2 * HEAD), bf16)
    dma = pltpu.SemaphoreType.DMA
    vmem = pl.BlockSpec(memory_space=pltpu.VMEM)
    wide = weight.shape[1]
    own = pltpu.VMEM((2, BLOCK, 2 * HEAD), bf16)
    eighth = pltpu.VMEM((ITEMS, BLOCK, HEAD), bf16)
    return pl.pallas_call(
        layer_kernel,
        name="layer",
        out_shape=(
            jax.ShapeDtypeStruct((CHUNK, wide), bf16),
            home, home, home,
            jax.ShapeDtypeStruct((2 * HEAD, HEAD), f32),
            jax.ShapeDtypeStruct(sel.shape, jnp.int32),
        ),
        in_specs=[ANY] * 6,
        out_specs=(vmem, ANY, ANY, ANY, vmem, ANY),
        scratch_shapes=[
            own, own,
            pltpu.VMEM(weight.shape, bf16),
            pltpu.VMEM((2, BLOCK, wide), bf16),
            pltpu.SMEM(sel.shape, jnp.int32),
            eighth,
            pltpu.VMEM((ALL_BLOCKS, BLOCK, HEAD), bf16),
            pltpu.VMEM((ALL_BLOCKS, BLOCK, HEAD), bf16),
            eighth, eighth,
            pltpu.VMEM((ITEMS, SLOTS, BLOCK, BLOCK), bf16),
            pltpu.VMEM((ITEMS, SLOTS, BLOCK, HEAD), f32),
            pltpu.VMEM((ITEMS, 1, BLOCK), f32),
            pltpu.VMEM((2, 4, 2, 4, BLOCK, HEAD), bf16),
            pltpu.VMEM((2, 4, 4, BLOCK, HEAD), bf16),
            pltpu.VMEM((2, 2, 2, 2, BLOCK, HEAD), bf16),
            pltpu.VMEM((2, 2, 2, BLOCK, HEAD), bf16),
            own,
            pltpu.VMEM((DEPTH, 2, CHUNK, wide), bf16),
            pltpu.VMEM((DEPTH, CHUNK, wide), bf16),
            pltpu.VMEM((2, DEPTH // 2, CHUNK, wide), bf16),
            pltpu.VMEM((ROW, ROW, 2 * HEAD, HEAD), bf16),
            pltpu.VMEM((ROW, 2 * HEAD, HEAD), bf16),
            pltpu.VMEM((ROW - 1, ROW, 2 * HEAD, HEAD), bf16),
            pltpu.VMEM((ROW - 1, 2 * HEAD, HEAD), bf16),
            dma((4,)), dma, dma((5, 2)), dma((5, 2)),
            dma((2, 2, 2)), dma((2, 2, 2)), dma((2, 2)), dma((2, 2)),
            dma((2, 4, 2)), dma((2, 4, 2)), dma((4, 2)), dma((4, 2)),
            dma((2, 4)), dma((2, 4)), dma((2, 2, 2)), dma((2, 2, 2)), dma((2, 2)), dma((2, 2)),
            dma, dma, dma((2, 4)), dma((2, 4)), dma((3,)), dma((3,)), dma((3,)), dma((3,)),
        ],
        compiler_params=pltpu.CompilerParams(
            collective_id=0, has_side_effects=True, vmem_limit_bytes=VMEM_LIMIT
        ),
    )(q, k, v, sel, weight, cot)


def settle_kernel(*refs):
    count = len(refs) // 2
    for i in range(count):
        refs[count + i][...] = refs[i][...]


def settle(*arrays):
    vmem = pl.BlockSpec(memory_space=pltpu.VMEM)
    return pl.pallas_call(
        settle_kernel,
        name="settle",
        out_shape=tuple(jax.ShapeDtypeStruct(a.shape, a.dtype) for a in arrays),
        in_specs=[vmem] * len(arrays),
        out_specs=(vmem,) * len(arrays),
        compiler_params=pltpu.CompilerParams(vmem_limit_bytes=VMEM_LIMIT),
    )(*arrays)


def shards(queries, key_states, values, selection, out_weight, cotangent):
    def blocks(array):
        return array.reshape(2, BLOCK, -1)

    results = layer(
        blocks(queries), blocks(key_states), blocks(values), selection, out_weight,
        blocks(cotangent),
    )
    projected, query_grad, key_grad, value_grad, weight_grad = settle(*results[:5])
    query_grad, key_grad, value_grad = (
        g.reshape(queries.shape) for g in (query_grad, key_grad, value_grad)
    )
    return projected, query_grad, key_grad, value_grad, weight_grad


def solution(mesh):
    in_specs = (
        P("seq", "head"),
        P("seq", "head"),
        P("seq", "head"),
        P("head", "seq", None),
        P("head", None),
        P("seq", None),
    )
    out_specs = (
        P(("seq", "head"), None),
        P("seq", "head"),
        P("seq", "head"),
        P("seq", "head"),
        P("head", "seq"),
    )
    return jax.shard_map(shards, mesh=mesh, in_specs=in_specs, out_specs=out_specs, check_vma=False)
```

time: 155 us -> 128 us (0.83)
  Pallas kernels: 148 us -> 127 us
  matrix products: 4.57 us -> 0 us
    pallas_call x3 -> x1, Pallas kernels: 146 us -> 125 us  [layer(): pl.pallas_call(layer_kernel, name='layer', out_shape=(jax.ShapeDtypeStruc...]
    dot_general x1 -> x0, matrix products: 4.57 us -> none  [dot(): lax.dot_general(a, b, (contract, ((), ())), preferred_element_type=jnp.fl...]
where the time goes in v4:
time: 128 us
  Pallas kernels  127 us (99%)
    pallas_call x1, Pallas kernels, layer(): pl.pallas_call(layer_kernel, name='layer', out_shape=(jax.ShapeDtypeStruc...  125 us
    pallas_call x1, Pallas kernels, settle(): pl.pallas_call(settle_kernel, name='settle', out_shape=tuple((jax.ShapeDt...  2.75 us

profile of v4, /device:TPU:1, one launch (start us, length us, event | category | flops | bytes accessed | tf_op | source)
XLA Modules:
  0.0 128.0 jit_solution(14650025511253004748)
XLA Ops:
  0.6 124.6 %layer.1 = (bf16[64,2048]{1,0:T(8,128)(2,1)}, bf16[2,512,256]{2,1,0:T(8,128)(2,1)}, bf16[2,512,256]{2,1,0:T(8,128)(2,1)}, bf16[2,512,256]{2,1,0:T(8,128)(2,1)}, f32[256,128]{1,0:T(8,128)}, /*index=5*/s32[2,2,4]{2,1,0:T(2,128)}) custom-call(bf16[2,512,256]{2,1,0:T(8,128)(2,1)} %bitcast.8, bf16[2,512,256]{2,1,0:T(8,128)(2,1)} %bitcast.9, ...), custom_call_target="tpu_custom_call" | custom-call | tf_op jit(solution)/shard_map/layer/pallas_call | solution.py:580
  125.2 2.8 %settle.1 = (bf16[64,2048]{1,0:T(8,128)(2,1)}, bf16[2,512,256]{2,1,0:T(8,128)(2,1)}, bf16[2,512,256]{2,1,0:T(8,128)(2,1)}, bf16[2,512,256]{2,1,0:T(8,128)(2,1)}, f32[256,128]{1,0:T(8,128)}) custom-call(bf16[64,2048]{1,0:T(8,128)(2,1)} %get-tuple-element.15.refs_0_, bf16[2,512,256]{2,1,0:T(8,128)(2,1)} %get-tuple-element.16.refs_1_, ...), custom_call_target="tpu_custom_call" | custom-call | tf_op jit(solution)/shard_map/settle/pallas_call | solution.py:635

commit v5 on v4

--- a/solution.py
+++ b/solution.py
@@ -15,6 +15,7 @@
 SLOTS = 5
 ALL_BLOCKS = 32
 CHUNK = 64
+STEP = 256
 SHIFTS = (0, -1, 1, 2)
 SCALING = 1.0 / math.sqrt(HEAD)
 FACTOR = SCALING * math.log2(math.e)
@@ -122,29 +123,29 @@
 
     home_at = 4 * (2 * y + x // 2) + 2 * odd
 
-    def row_refs(t, h):
+    def row_refs(t, h, b):
         cols = pl.ds(h * HEAD, HEAD)
         if t == 0:
-            return k_own.at[:, :, cols], kn.at[pl.ds(home_at, 2)]
+            return k_own.at[pl.ds(b, 1), :, cols], kn.at[pl.ds(home_at + b, 1)]
         if t == 1:
             return q_in.at[:, :, cols], qn.at[pl.ds(2 * odd, 2)]
         if t == 2:
-            return v_own.at[:, :, cols], vn.at[pl.ds(home_at, 2)]
+            return v_own.at[pl.ds(b, 1), :, cols], vn.at[pl.ds(home_at + b, 1)]
         if t == 3:
             return k_own.at[:, :, cols], don.at[pl.ds(2 * odd, 2)]
         return sel_in.at[h], sel_land.at[odd]
 
-    def row_go(t):
+    def row_go(t, b=0):
         for h in range(2):
-            src, dst = row_refs(t, h)
-            row_start(src, dst, row_send.at[t, h], row_recv.at[t, odd], h)
-
-    def row_sent(t):
+            src, dst = row_refs(t, h, b)
+            row_start(src, dst, row_send.at[t, h, b], row_recv.at[t, odd, b], h)
+
+    def row_sent(t, b=0):
         for h in range(2):
-            src, dst = row_refs(t, h)
-            row_wait_send(src, dst, row_send.at[t, h], row_recv.at[t, odd], h)
-
-    def row_arrive(t, j):
+            src, dst = row_refs(t, h, b)
+            row_wait_send(src, dst, row_send.at[t, h, b], row_recv.at[t, odd, b], h)
+
+    def row_arrive(t, j, b=0):
         if t == 1:
             dst = qn.at[pl.ds(2 * j, 2)]
         elif t == 3:
@@ -152,54 +153,59 @@
         elif t == 4:
             dst = sel_land.at[j]
         else:
-            dst = piece(t // 2, 0, c, j)
-        row_wait_recv(dst, row_recv.at[t, j])
-
-    def piece(t, shift, core, j):
+            dst = piece(t // 2, 0, c, j, b)
+        row_wait_recv(dst, row_recv.at[t, j, b])
+
+    def piece(t, shift, core, j, b):
         quarter = lax.rem(y + shift + ROW, ROW)
-        return (kn, vn)[t].at[pl.ds(4 * (2 * quarter + core) + 2 * j, 2)]
-
-    def kv_sib(t, m, j):
-        own = piece(t, SHIFTS[m], c, j)
-        return remote(own, own, kv_sib_send.at[t, m, j], kv_sib_recv.at[t, m, j], sibling)
-
-    def kv_ring(t, way, j):
-        own = piece(t, 0, c, j)
-        return remote(own, own, kv_send.at[t, way, j], kv_recv.at[t, way, j], (up, down)[way])
-
-    def kv_far(t, way):
-        own = piece(t, (-1, 1)[way], c, way)
-        return remote(
-            own, own, kv_far_send.at[t, way], kv_far_recv.at[t, way], (up, down)[way]
-        )
-
-    def kv_begin(t):
+        return (kn, vn)[t].at[pl.ds(4 * (2 * quarter + core) + 2 * j + b, 1)]
+
+    def kv_sib(t, m, j, b):
+        own = piece(t, SHIFTS[m], c, j, b)
+        return remote(
+            own, own, kv_sib_send.at[t, m, j, b], kv_sib_recv.at[t, m, j, b], sibling
+        )
+
+    def kv_ring(t, way, j, b):
+        own = piece(t, 0, c, j, b)
+        return remote(
+            own, own, kv_send.at[t, way, j, b], kv_recv.at[t, way, j, b], (up, down)[way]
+        )
+
+    def kv_far(t, way, b):
+        own = piece(t, (-1, 1)[way], c, way, b)
+        return remote(
+            own, own, kv_far_send.at[t, way, b], kv_far_recv.at[t, way, b], (up, down)[way]
+        )
+
+    def kv_begin(t, b):
         for j in range(2):
-            row_arrive(2 * t, j)
-            kv_ring(t, j, j).start()
-            kv_ring(t, 1 - j, j).start()
-            kv_sib(t, 0, j).start()
-
-    def kv_relay(t):
-        for way in range(2):
-            kv_ring(t, way, way).wait_recv()
-            kv_far(t, way).start()
-            kv_sib(t, 1 + way, way).start()
-
-    def kv_rest(t):
-        for way in range(2):
-            kv_ring(t, way, 1 - way).wait_recv()
-            kv_sib(t, 1 + way, 1 - way).start()
-
-    def kv_last(t):
-        for way in range(2):
-            kv_far(t, way).wait_recv()
-            kv_sib(t, 3, way).start()
+            row_arrive(2 * t, j, b)
+            kv_ring(t, j, j, b).start()
+            kv_ring(t, 1 - j, j, b).start()
+            kv_sib(t, 0, j, b).start()
+
+    def kv_relay(t, b):
+        for way in range(2):
+            kv_ring(t, way, way, b).wait_recv()
+            kv_far(t, way, b).start()
+            kv_sib(t, 1 + way, way, b).start()
+
+    def kv_rest(t, b):
+        for way in range(2):
+            kv_ring(t, way, 1 - way, b).wait_recv()
+            kv_sib(t, 1 + way, 1 - way, b).start()
+
+    def kv_last(t, b):
+        for way in range(2):
+            kv_far(t, way, b).wait_recv()
+            kv_sib(t, 3, way, b).start()
 
     def kv_end(t):
         for m in range(4):
             for j in range(2):
-                kv_sib(t, m, j).wait_recv()
+                for b in range(2):
+                    kv_sib(t, m, j, b).wait_recv()
 
     def gradient_rows(lo, hi):
         @pl.loop(lo, hi)
@@ -210,53 +216,68 @@
 
     out, dq = don, scaled
 
-    def item_ids(item):
-        block = 8 * y + 4 * c + item
-        return block, [sel[item // 2, item % 2, t] for t in range(SLOTS - 1)]
+    def item_block(item):
+        return 8 * y + 4 * c + item
+
+    def chosen_id(item, t):
+        return sel[item // 2, item % 2, t - 1]
+
+    def slot_id(item, t):
+        return jnp.where(t == 0, item_block(item), chosen_id(item, jnp.maximum(t, 1)))
 
     def weigh(lo, hi):
         @pl.loop(lo, hi)
         def _(item):
-            block, ids = item_ids(item)
+            block = item_block(item)
             query_t = qn[item].T
-            top = jnp.full((1, BLOCK), -1e30, f32)
-            for t in range(SLOTS):
-                if t == 0:
-                    s = dot(kn[block], query_t, ((1,), (0,)))
-                    key_at = lax.broadcasted_iota(jnp.int32, (BLOCK, BLOCK), 0)
-                    query_at = lax.broadcasted_iota(jnp.int32, (BLOCK, BLOCK), 1)
-                    s = jnp.where(key_at <= query_at, s, -1e30)
-                else:
-                    s = dot(kn[ids[t - 1]], query_t, ((1,), (0,)))
-                    s = jnp.where(ids[t - 1] < block, s, -1e30)
+
+            def keep(s, t):
                 for n in range(ITEMS):
                     terms[n, t] = s[:, n * HEAD : (n + 1) * HEAD]
-                top = jnp.maximum(top, jnp.max(s, axis=0, keepdims=True))
-            top = top * FACTOR
-            total = jnp.zeros((1, BLOCK), f32)
-            for t in range(SLOTS):
-                s = jnp.concatenate([terms[n, t] for n in range(ITEMS)], axis=1)
-                e = jnp.exp2(s * FACTOR - top)
-                total = total + jnp.sum(e, axis=0, keepdims=True)
-                expons[item, t] = e.astype(bf16)
-            stats[item] = 1.0 / total
+                return jnp.max(s, axis=0, keepdims=True)
+
+            s = dot(kn[block], query_t, ((1,), (0,)))
+            key_at = lax.broadcasted_iota(jnp.int32, (BLOCK, BLOCK), 0)
+            query_at = lax.broadcasted_iota(jnp.int32, (BLOCK, BLOCK), 1)
+            top = keep(jnp.where(key_at <= query_at, s, -1e30), 0)
+
+            def score(t, top):
+                at = chosen_id(item, t)
+                s = dot(kn[at], query_t, ((1,), (0,)))
+                return jnp.maximum(top, keep(jnp.where(at < block, s, -1e30), t))
+
+            top = lax.fori_loop(1, SLOTS, score, top) * FACTOR
+
+            def exponentiate(t, total):
+                sums = []
+                for n in range(ITEMS):
+                    cols = slice(n * HEAD, (n + 1) * HEAD)
+                    e = jnp.exp2(terms[n, t] * FACTOR - top[:, cols])
+                    sums.append(jnp.sum(e, axis=0, keepdims=True))
+                    expons[item, t, :, cols] = e.astype(bf16)
+                return total + jnp.concatenate(sums, axis=1)
+
+            stats[item] = 1.0 / lax.fori_loop(
+                0, SLOTS, exponentiate, jnp.zeros((1, BLOCK), f32)
+            )
 
     def value_terms():
         @pl.loop(0, ITEMS)
         def _(item):
             scaled_t = (don[item].T.astype(f32) * stats[item]).astype(bf16)
             scaled[item] = scaled_t.T
-            rows = scaled[item]
-            for t in range(SLOTS):
-                terms[item, t] = dot(expons[item, t], rows, ((1,), (0,)))
+
+            @pl.loop(0, SLOTS)
+            def _(t):
+                terms[item, t] = dot(expons[item, t], scaled[item], ((1,), (0,)))
 
     def attend():
         @pl.loop(0, ITEMS)
         def _(item):
-            block, ids = item_ids(item)
-            out_t = dot(vn[block], expons[item, 0], ((0,), (0,)))
-            for t in range(1, SLOTS):
-                out_t = out_t + dot(vn[ids[t - 1]], expons[item, t], ((0,), (0,)))
+            def add(t, out_t):
+                return out_t + dot(vn[slot_id(item, t)], expons[item, t], ((0,), (0,)))
+
+            out_t = lax.fori_loop(0, SLOTS, add, jnp.zeros((HEAD, BLOCK), f32))
             out_t = (out_t * stats[item]).astype(bf16)
             product = don[item].T.astype(f32) * out_t.astype(f32)
             out[item] = out_t.T
@@ -265,17 +286,21 @@
     def backward(lo, hi):
         @pl.loop(lo, hi)
         def _(item):
-            block, ids = item_ids(item)
             query = qn[item]
             scaled_t = scaled[item].T
             delta = stats[item]
-            dq_t = jnp.zeros((HEAD, BLOCK), f32)
-            for t in range(SLOTS):
-                at = block if t == 0 else ids[t - 1]
-                dp = dot(vn[at], scaled_t, ((1,), (0,)))
-                ds = (expons[item, t].astype(f32) * (dp - delta)).astype(bf16)
-                dq_t = dq_t + dot(kn[at], ds, ((0,), (0,)))
-                terms[item, t] = dot(ds, query, ((1,), (0,)))
+
+            def add(t, dq_t):
+                at = slot_id(item, t)
+                for n in range(BLOCK // STEP):
+                    rows = slice(n * STEP, (n + 1) * STEP)
+                    dp = dot(vn[at, rows, :], scaled_t, ((1,), (0,)))
+                    ds = (expons[item, t, rows, :].astype(f32) * (dp - delta)).astype(bf16)
+                    dq_t = dq_t + dot(kn[at, rows, :], ds, ((0,), (0,)))
+                    terms[item, t, rows, :] = dot(ds, query, ((1,), (0,)))
+                return dq_t
+
+            dq_t = lax.fori_loop(0, SLOTS, add, jnp.zeros((HEAD, BLOCK), f32), unroll=True)
             dq[item] = (dq_t * SCALING).astype(bf16).T
 
     def gather_terms(t, m):
@@ -284,10 +309,10 @@
             target = 8 * lax.rem(y + SHIFTS[m] + ROW, ROW) + i
             total = jnp.zeros((BLOCK, HEAD), f32)
             for item in range(ITEMS):
-                block, ids = item_ids(item)
+                block = item_block(item)
                 slot = jnp.int32(0)
-                for s in range(SLOTS - 1):
-                    slot = jnp.where(ids[s] == target, s + 1, slot)
+                for s in range(1, SLOTS):
+                    slot = jnp.where(chosen_id(item, s) == target, s, slot)
                 slot = jnp.where(target == block, 0, slot)
                 chosen = (target == block) | (slot > 0)
                 total = total + jnp.where(chosen, terms[item, slot], 0.0)
@@ -328,8 +353,8 @@
             ring_send.at[t, way, j], ring_recv.at[t, way, j], (up, down)[way],
         )
 
-    def share(t):
-        for m in (3, 1, 2, 0):
+    def share(t, *shifts):
+        for m in shifts:
             gather_terms(t, m)
             sib_copy(t, m).start()
 
@@ -481,21 +506,33 @@
         weight_grad[...] = total
 
     loads[0].wait()
-    row_go(0)
+    row_go(0, 0)
     loads[1].wait()
-    kv_begin(0)
-    row_go(2)
-    row_sent(0)
+    row_sent(0, 0)
+    row_go(0, 1)
+    kv_begin(0, 0)
+    row_sent(0, 1)
+    row_go(2, 0)
+    kv_begin(0, 1)
     loads[2].wait()
     loads[3].wait()
-    gradient_rows(0, 4)
-    kv_relay(0)
+    gradient_rows(0, 2)
+    kv_relay(0, 0)
+    row_sent(2, 0)
+    row_go(2, 1)
+    gradient_rows(2, 4)
+    kv_relay(0, 1)
+    kv_rest(0, 0)
+    row_sent(2, 1)
     row_go(1)
     row_go(4)
-    kv_rest(0)
+    kv_rest(0, 1)
+    kv_last(0, 0)
+    kv_begin(1, 0)
+    row_sent(1)
     row_go(3)
-    kv_last(0)
-    kv_begin(1)
+    kv_last(0, 1)
+    kv_begin(1, 1)
     for j in range(2):
         row_arrive(4, j)
     sel_copy = pltpu.make_async_copy(sel_land, sel, sel_sem)
@@ -504,48 +541,53 @@
         row_arrive(1, j)
     kv_end(0)
     sel_copy.wait()
-    weigh(0, 4)
-    kv_relay(1)
-    kv_rest(1)
+    weigh(0, 3)
+    kv_relay(1, 0)
+    kv_relay(1, 1)
+    weigh(3, 4)
+    kv_rest(1, 0)
+    kv_rest(1, 1)
     for j in range(2):
         row_arrive(3, j)
     value_terms()
-    share(1)
-    kv_last(1)
+    share(1, 3, 1)
     back_far(1)
+    share(1, 2, 0)
+    kv_last(1, 0)
+    kv_last(1, 1)
     kv_end(1)
     attend()
     for j in range(2):
         go_home(3, j)
     back_near(1)
-    backward(0, 1)
+    backward(0, 2)
+    go_home(2, 0)
     back_sum(1)
     come_home(3)
     project()
-    backward(1, 2)
+    backward(2, 3)
     project_sum()
-    backward(2, 3)
+    backward(3, 4)
+    go_home(2, 1)
+    share(0, 3, 1)
+    back_far(0)
+    share(0, 2, 0)
     z_step(3)
-    backward(3, 4)
-    share(0)
-    back_far(0)
-    for j in range(2):
-        go_home(2, j)
+    back_near(0)
+    back_end(1)
+    weight_start()
     z_step(2)
-    back_near(0)
-    weight_start()
     back_sum(0)
     z_step(1)
+    back_end(0)
     weight_middle()
-    back_end(1)
     project_end()
     weight_end()
-    back_end(0)
 
     for t in range(3):
         come_home(t)
-    for t in range(1, 5):
-        row_sent(t)
+    row_sent(3)
+    row_sent(4)
     for t in range(4):
         for j in range(2):
             src, dst = home_refs(t, j)
@@ -554,13 +596,15 @@
         for m in range(4):
             sib_copy(t, m).wait_send()
             for j in range(2):
-                kv_sib(t, m, j).wait_send()
+                for b in range(2):
+                    kv_sib(t, m, j, b).wait_send()
         for way in range(2):
             far_copy(t, way).wait_send()
-            kv_far(t, way).wait_send()
             for j in range(2):
                 ring_copy(t, way, j).wait_send()
-                kv_ring(t, way, j).wait_send()
+                kv_far(t, way, j).wait_send()
+                for b in range(2):
+                    kv_ring(t, way, j, b).wait_send()
     for step in range(1, DEPTH // 2 + 1):
         for way in range(2):
             z_copy(way, step).wait_send()
@@ -612,9 +656,9 @@
             pltpu.VMEM((ROW, 2 * HEAD, HEAD), bf16),
             pltpu.VMEM((ROW - 1, ROW, 2 * HEAD, HEAD), bf16),
             pltpu.VMEM((ROW - 1, 2 * HEAD, HEAD), bf16),
-            dma((4,)), dma, dma((5, 2)), dma((5, 2)),
-            dma((2, 2, 2)), dma((2, 2, 2)), dma((2, 2)), dma((2, 2)),
-            dma((2, 4, 2)), dma((2, 4, 2)), dma((4, 2)), dma((4, 2)),
+            dma((4,)), dma, dma((5, 2, 2)), dma((5, 2, 2)),
+            dma((2, 2, 2, 2)), dma((2, 2, 2, 2)), dma((2, 2, 2)), dma((2, 2, 2)),
+            dma((2, 4, 2, 2)), dma((2, 4, 2, 2)), dma((4, 2)), dma((4, 2)),
             dma((2, 4)), dma((2, 4)), dma((2, 2, 2)), dma((2, 2, 2)), dma((2, 2)), dma((2, 2)),
             dma, dma, dma((2, 4)), dma((2, 4)), dma((3,)), dma((3,)), dma((3,)), dma((3,)),
         ],

time: 128 us -> 123 us (0.961)
  Pallas kernels: 127 us -> 122 us
    pallas_call x1, Pallas kernels: 125 us -> 119 us  [layer(): pl.pallas_call(layer_kernel, name='layer', out_shape=(jax.ShapeDtypeStruc...]
where the time goes in v5:
time: 123 us; the launch traced here: 122 us
  Pallas kernels  122 us (99%)
    pallas_call x1, Pallas kernels, layer(): pl.pallas_call(layer_kernel, name='layer', out_shape=(jax.ShapeDtypeStruc...  119 us
    pallas_call x1, Pallas kernels, settle(): pl.pallas_call(settle_kernel, name='settle', out_shape=tuple((jax.ShapeDt...  2.75 us

profile of v5, /device:TPU:1, one launch (start us, length us, event | category | flops | bytes accessed | tf_op | source)
XLA Modules:
  0.0 122.4 jit_solution(10879883596618903493)
XLA Ops:
  0.6 119.0 %layer.1 = (bf16[64,2048]{1,0:T(8,128)(2,1)}, bf16[2,512,256]{2,1,0:T(8,128)(2,1)}, bf16[2,512,256]{2,1,0:T(8,128)(2,1)}, bf16[2,512,256]{2,1,0:T(8,128)(2,1)}, f32[256,128]{1,0:T(8,128)}, /*index=5*/s32[2,2,4]{2,1,0:T(2,128)}) custom-call(bf16[2,512,256]{2,1,0:T(8,128)(2,1)} %bitcast.8, bf16[2,512,256]{2,1,0:T(8,128)(2,1)} %bitcast.9, ...), custom_call_target="tpu_custom_call" | custom-call | tf_op jit(solution)/shard_map/layer/pallas_call | solution.py:624
  119.7 2.8 %settle.1 = (bf16[64,2048]{1,0:T(8,128)(2,1)}, bf16[2,512,256]{2,1,0:T(8,128)(2,1)}, bf16[2,512,256]{2,1,0:T(8,128)(2,1)}, bf16[2,512,256]{2,1,0:T(8,128)(2,1)}, f32[256,128]{1,0:T(8,128)}) custom-call(bf16[64,2048]{1,0:T(8,128)(2,1)} %get-tuple-element.15.refs_0_, bf16[2,512,256]{2,1,0:T(8,128)(2,1)} %get-tuple-element.16.refs_1_, ...), custom_call_target="tpu_custom_call" | custom-call | tf_op jit(solution)/shard_map/settle/pallas_call | solution.py:679

commit v6 on v5

--- a/solution.py
+++ b/solution.py
@@ -267,7 +267,7 @@
             scaled_t = (don[item].T.astype(f32) * stats[item]).astype(bf16)
             scaled[item] = scaled_t.T
 
-            @pl.loop(0, SLOTS)
+            @pl.loop(0, SLOTS, unroll=True)
             def _(t):
                 terms[item, t] = dot(expons[item, t], scaled[item], ((1,), (0,)))
 
@@ -277,7 +277,7 @@
             def add(t, out_t):
                 return out_t + dot(vn[slot_id(item, t)], expons[item, t], ((0,), (0,)))
 
-            out_t = lax.fori_loop(0, SLOTS, add, jnp.zeros((HEAD, BLOCK), f32))
+            out_t = lax.fori_loop(0, SLOTS, add, jnp.zeros((HEAD, BLOCK), f32), unroll=True)
             out_t = (out_t * stats[item]).astype(bf16)
             product = don[item].T.astype(f32) * out_t.astype(f32)
             out[item] = out_t.T

time: 123 us -> 116 us (0.943)
  Pallas kernels: 122 us -> 116 us
    pallas_call x1, Pallas kernels: 119 us -> 113 us  [layer(): pl.pallas_call(layer_kernel, name='layer', out_shape=(jax.ShapeDtypeStruc...]
where the time goes in v6:
time: 116 us
  Pallas kernels  116 us (100%)
    pallas_call x1, Pallas kernels, layer(): pl.pallas_call(layer_kernel, name='layer', out_shape=(jax.ShapeDtypeStruc...  113 us
    pallas_call x1, Pallas kernels, settle(): pl.pallas_call(settle_kernel, name='settle', out_shape=tuple((jax.ShapeDt...  2.75 us

profile of v6, /device:TPU:1, one launch (start us, length us, event | category | flops | bytes accessed | tf_op | source)
XLA Modules:
  0.0 116.3 jit_solution(10811687902806446961)
XLA Ops:
  0.6 112.9 %layer.1 = (bf16[64,2048]{1,0:T(8,128)(2,1)}, bf16[2,512,256]{2,1,0:T(8,128)(2,1)}, bf16[2,512,256]{2,1,0:T(8,128)(2,1)}, bf16[2,512,256]{2,1,0:T(8,128)(2,1)}, f32[256,128]{1,0:T(8,128)}, /*index=5*/s32[2,2,4]{2,1,0:T(2,128)}) custom-call(bf16[2,512,256]{2,1,0:T(8,128)(2,1)} %bitcast.8, bf16[2,512,256]{2,1,0:T(8,128)(2,1)} %bitcast.9, ...), custom_call_target="tpu_custom_call" | custom-call | tf_op jit(solution)/shard_map/layer/pallas_call | solution.py:624
  113.6 2.8 %settle.1 = (bf16[64,2048]{1,0:T(8,128)(2,1)}, bf16[2,512,256]{2,1,0:T(8,128)(2,1)}, bf16[2,512,256]{2,1,0:T(8,128)(2,1)}, bf16[2,512,256]{2,1,0:T(8,128)(2,1)}, f32[256,128]{1,0:T(8,128)}) custom-call(bf16[64,2048]{1,0:T(8,128)(2,1)} %get-tuple-element.15.refs_0_, bf16[2,512,256]{2,1,0:T(8,128)(2,1)} %get-tuple-element.16.refs_1_, ...), custom_call_target="tpu_custom_call" | custom-call | tf_op jit(solution)/shard_map/settle/pallas_call | solution.py:679
